TPU v7x, 32 devices: a whole 2x2x4 slice. The times are simulated.
32 devices in a mesh: seq: 16 (over z, y, x), heads: 2 (over core).
Axes of the slice: x: 2, y: 2, z: 4, core: 2. Of those that a mesh axis runs over, the one named last changes fastest.
Arguments:
- queries: bfloat16 [2048, 24576], P('seq', 'heads'), may hold values from -8 to 8
- latent: bfloat16 [2048, 576], P(('seq', 'heads')), may hold values from -8 to 8
- w_uk: bfloat16 [128, 128, 512], P('heads'), may hold values from -0.5 to 0.5
- w_uv: bfloat16 [128, 512, 128], P('heads'), may hold values from -0.75 to 0.75
- doc_lengths: int32 [8], replicated, may hold values from 1 to 1024, as said below
Outputs:
- attention_out: bfloat16 [2048, 16384], P('seq', 'heads')
Inputs may be any that keep to these rules, and one draw needn't show every extreme that they name: `doc_lengths`: the 8 lengths sum to 2048; the next to last document has exactly 1024 tokens and the last one at most 32.
All inputs are finite; a program needn't handle non-finite values.
Results may differ from a plain program's by a relative error of at most 0.0085.
Values may be sent and summed in bfloat16 or wider, within the bound.
No kernel may reach another device: no remote copies, remote signals or barrier semaphores. Data moves between devices by JAX's collectives and lax.ppermute only.
A program may use at most 320 MiB of HBM per device.

v0:
```python
import jax
import jax.numpy as jnp
from jax import lax
from jax.sharding import PartitionSpec as P

SPAN = 8


far_negative = -1e30


def from_behind(x, axis, by):
    length = lax.axis_size(axis)
    pairs = [(i, i + by) for i in range(length) if 0 <= i + by < length]
    return lax.ppermute(x, axis, pairs)


def document_of(doc_ends, positions):
    return jnp.sum((doc_ends[None, :] <= positions[:, None]).astype(jnp.int32), axis=1)


def reach_back(own_block):
    held = own_block[None]
    stride = 1
    while stride < SPAN:
        held = jnp.concatenate([from_behind(held, "seq", stride), held], axis=0)
        stride = stride * 2
    farthest = from_behind(own_block, "seq", SPAN)
    return jnp.concatenate([farthest[None], held], axis=0)


def per_device(queries, latent, w_uk, w_uv, doc_lengths):
    heads_dev, nope_width, latent_rank = w_uk.shape
    value_width = w_uv.shape[2]
    tok_rows = queries.shape[0]
    query_width = queries.shape[1] // heads_dev
    score_scale = query_width ** (-0.5)
    query_heads = queries.reshape(tok_rows, heads_dev, query_width)
    absorbed = jnp.einsum(
        "thd,hdl->thl", query_heads[:, :, :nope_width], w_uk, preferred_element_type=jnp.float32
    ).astype(jnp.bfloat16)
    joined = jnp.concatenate([absorbed, query_heads[:, :, nope_width:]], axis=2)
    own_rows = lax.all_gather(latent, "heads", axis=0, tiled=True)
    window = reach_back(own_rows)
    first_pos = lax.axis_index("seq") * tok_rows
    doc_ends = jnp.cumsum(doc_lengths)
    query_pos = first_pos + jnp.arange(tok_rows, dtype=jnp.int32)
    key_pos = first_pos - SPAN * tok_rows + jnp.arange((SPAN + 1) * tok_rows, dtype=jnp.int32)
    query_doc = document_of(doc_ends, query_pos)
    key_doc = document_of(doc_ends, key_pos)
    allowed = (
        (key_doc[None, :] == query_doc[:, None])
        & (key_pos[None, :] <= query_pos[:, None])
        & (key_pos[None, :] >= 0)
    )
    allowed = allowed.reshape(tok_rows, SPAN + 1, tok_rows)
    value_rows = window[:, :, :latent_rank]
    raw_scores = jnp.einsum("thl,jkl->thjk", joined, window, preferred_element_type=jnp.float32)
    scores = jnp.where(allowed[:, None], raw_scores * score_scale, far_negative)
    row_top = jnp.max(scores, axis=(2, 3), keepdims=True)
    exponent = jnp.exp(scores - row_top)
    row_total = jnp.sum(exponent, axis=(2, 3))
    weights = exponent.astype(jnp.bfloat16)
    mixed_sum = jnp.einsum("thjk,jkl->thl", weights, value_rows, preferred_element_type=jnp.float32)
    attended = (mixed_sum / row_total[:, :, None]).astype(jnp.bfloat16)
    projected = jnp.einsum("thl,hlv->thv", attended, w_uv, preferred_element_type=jnp.float32)
    return projected.astype(jnp.bfloat16).reshape(tok_rows, heads_dev * value_width)


def solution(mesh):
    return jax.shard_map(
        per_device,
        mesh=mesh,
        in_specs=(
            P("seq", "heads"),
            P(("seq", "heads"), None),
            P("heads", None, None),
            P("heads", None, None),
            P(),
        ),
        out_specs=P("seq", "heads"),
        check_vma=False,
    )
```

profile of v0, /device:TPU:0, one launch (start us, length us, event | category | flops | bytes accessed | tf_op | source)
XLA Modules:
  0.0 120.7 jit_solution(5909068044055918589)
XLA Ops:
  0.0 2.2 %all_gather.3 = bf16[128,576]{1,0:T(8,128)(2,1)S(1)} all-gather(bf16[64,576]{1,0:T(8,128)(2,1)} %param.6), channel_id=1, replica_groups=mesh['seq'=16,'heads'=2] {'heads'}, dimensions={0}, use_global_device_ids=true | all-gather | bytes 221184 | tf_op jit(solution)/shard_map/all_gather | solution.py:43
  2.2 0.1 copy.26
  2.4 6.5 %collective-permute-start = (bf16[128,576]{0,1:T(8,128)(2,1)S(1)}, bf16[128,576]{0,1:T(8,128)(2,1)}, u32[]{:S(2)}, u32[]{:S(2)}) collective-permute-start(bf16[128,576]{0,1:T(8,128)(2,1)S(1)} %copy.26), channel_id=1, source_target_pairs={{0,16},{2,18},{4,20},{6,22},{8,24},{10,26},{12,28},{14,30},{1,17},... | collective-permute-start | bytes 442376 | tf_op jit(solution)/shard_map/ppermute | solution.py:15
  8.9 3.4 %collective-permute-start.1 = (bf16[1,128,576]{1,2,0:T(8,128)(2,1)S(1)}, bf16[1,128,576]{1,2,0:T(8,128)(2,1)S(1)}, u32[]{:S(2)}, u32[]{:S(2)}) collective-permute-start(bf16[1,128,576]{1,2,0:T(8,128)(2,1)S(1)} %bitcast.42), channel_id=1, source_target_pairs={{0,2},{2,4},{4,6},{6,8},{8,10},{10,12},{12,14},{14,16},{16,18},{18... | collective-permute-start | bytes 442376 | tf_op jit(solution)/shard_map/ppermute | solution.py:15
  12.3 3.5 %copy.23 = bf16[128,12288]{0,1:T(8,128)(2,1)S(1)} copy(bf16[128,12288]{1,0:T(8,128)(2,1)} %param.5) | data formatting | bytes 6291456 | tf_op args[0]
  15.8 0.0 copy-start.1
  15.8 9.0 %convert_bitcast_fusion = bf16[128,64,512]{0,2,1:T(8,128)(2,1)} fusion(bf16[64,128,512]{2,1,0:T(8,128)(2,1)} %param.7, bf16[128,64,192]{0,2,1:T(8,128)(2,1)S(1)} %bitcast.40), kind=kOutput, calls=%fused_computation.17 | convolution fusion | flops 1077936128 | bytes 18874368 | tf_op jit(solution)/shard_map/thd,hdl->thl/dot_general | solution.py:39
  24.8 0.0 copy-done.1
  24.8 0.2 reduce-window.8
  25.0 0.0 collective-permute-done.1
  25.0 3.4 %collective-permute-start.2 = (bf16[2,128,576]{1,2,0:T(8,128)(2,1)S(1)}, bf16[2,128,576]{1,2,0:T(8,128)(2,1)S(1)}, u32[]{:S(2)}, u32[]{:S(2)}) collective-permute-start(bf16[2,128,576]{1,2,0:T(8,128)(2,1)S(1)} %pad_maximum_fusion.1), channel_id=1, source_target_pairs={{0,4},{2,6},{4,8},{6,10},{8,12},{10,14},{12,16},{14,18},{16,20},{1... | collective-permute-start | bytes 884744 | tf_op jit(solution)/shard_map/ppermute | solution.py:15
  28.5 0.1 convert_reduce_fusion.1
  28.6 5.9 %collective-permute-done.2 = bf16[2,128,576]{1,2,0:T(8,128)(2,1)S(1)} collective-permute-done((bf16[2,128,576]{1,2,0:T(8,128)(2,1)S(1)}, bf16[2,128,576]{1,2,0:T(8,128)(2,1)S(1)}, u32[]{:S(2)}, u32[]{:S(2)}) %collective-permute-start.2) | collective-permute-done | bytes 294944 | tf_op jit(solution)/shard_map/ppermute | solution.py:15
  34.4 0.1 pad_maximum_fusion
  34.5 5.6 %collective-permute-start.3 = (bf16[4,128,576]{1,2,0:T(8,128)(2,1)S(1)}, bf16[4,128,576]{1,2,0:T(8,128)(2,1)S(1)}, u32[]{:S(2)}, u32[]{:S(2)}) collective-permute-start(bf16[4,128,576]{1,2,0:T(8,128)(2,1)S(1)} %pad_maximum_fusion), channel_id=1, source_target_pairs={{0,8},{2,10},{4,12},{6,14},{8,16},{10,18},{12,20},{14,22},{16,24},... | collective-permute-start | bytes 1769480 | tf_op jit(solution)/shard_map/ppermute | solution.py:15
  40.1 0.1 slice.13
  40.2 0.1 convert_reduce_fusion
  40.3 0.7 and_and_fusion
  41.0 0.0 collective-permute-done
  41.0 0.9 bitcast_dynamic-update-slice_fusion
  41.9 9.4 %collective-permute-done.3 = bf16[4,128,576]{1,2,0:T(8,128)(2,1)S(1)} collective-permute-done((bf16[4,128,576]{1,2,0:T(8,128)(2,1)S(1)}, bf16[4,128,576]{1,2,0:T(8,128)(2,1)S(1)}, u32[]{:S(2)}, u32[]{:S(2)}) %collective-permute-start.3) | collective-permute-done | bytes 589856 | tf_op jit(solution)/shard_map/ppermute | solution.py:15
  51.3 0.1 constant_dynamic-update-slice_fusion.3
  51.5 0.0 copy-start
  51.5 25.6 %fusion = (f32[128,64]{0,1:T(8,128)S(1)}, f32[128,64,9,128]{0,3,2,1:T(8,128)}) fusion(pred[128,9,128]{0,2,1:T(8,128)(4,1)S(1)} %and_and_fusion, bf16[9,128,576]{1,2,0:T(8,128)(2,1)S(1)} %constant_dynamic-update-slice_fusion, bf16[128,64,64]{0,2,1:T(8,128)(2,1)S(1)} %slice.13, bf16[128,64,512]{0,2,1:T(8,128)(2,1)} %convert_bitcast_fusion), kind=kOutput, calls=%fused_computation.2 | convolution fusion | flops 10918813696 | bytes 48693248 | tf_op jit(solution)/shard_map/thl,jkl->thjk/dot_general | solution.py:58
  77.1 0.0 copy-done
  77.1 16.6 %fusion.1 = f32[128,64]{0,1:T(8,128)S(1)} fusion(f32[128,64,9,128]{0,3,2,1:T(8,128)} %get-tuple-element.6, f32[128,64]{0,1:T(8,128)S(1)} %get-tuple-element.5, pred[128,9,128]{0,2,1:T(8,128)(4,1)S(1)} %and_and_fusion), kind=kLoop, calls=%fused_computation.3 | loop fusion | flops 37740544 | bytes 37961728 | tf_op jit(solution)/shard_map/reduce_sum | solution.py:62
  93.6 24.1 %fusion.19 = bf16[64,128,128]{1,2,0:T(8,128)(2,1)S(1)} fusion(bf16[64,512,128]{2,1,0:T(8,128)(2,1)} %param.8, f32[128,64,9,128]{0,3,2,1:T(8,128)} %get-tuple-element.6, f32[128,64]{0,1:T(8,128)S(1)} %get-tuple-element.5, pred[128,9,128]{0,2,1:T(8,128)(4,1)S(1)} %and_and_fusion, f32[128,64]{0,1:T(8,128)S(1)} %fusion.1, bf16[9,128,576]{1,2,0:T(8,128)(2,1)} %copy-done), kind=kOutput, calls=%fused_computation.19 | convolution fusion | flops 10784604160 | bytes 49627136 | tf_op jit(solution)/shard_map/thl,hlv->thv/dot_general | solution.py:66
  117.8 2.9 %copy.31 = bf16[128,8192]{1,0:T(8,128)(2,1)} copy(bf16[128,8192]{0,1:T(8,128)(2,1)S(1)} %bitcast.45) | data formatting | bytes 4194304 | tf_op jit(solution)/shard_map/reshape | solution.py:67
  (8 shorter events, 0.1 us)
Async XLA Ops:
  2.4 38.6 %collective-permute-start = (bf16[128,576]{0,1:T(8,128)(2,1)S(1)}, bf16[128,576]{0,1:T(8,128)(2,1)}, u32[]{:S(2)}, u32[]{:S(2)}) collective-permute-start(bf16[128,576]{0,1:T(8,128)(2,1)S(1)} %copy.26), channel_id=1, source_target_pairs={{0,16},{2,18},{4,20},{6,22},{8,24},{10,26},{12,28},{14,30},{1,17},... | collective-permute-start | bytes 442376 | tf_op jit(solution)/shard_map/ppermute | solution.py:15
  8.9 16.1 %collective-permute-start.1 = (bf16[1,128,576]{1,2,0:T(8,128)(2,1)S(1)}, bf16[1,128,576]{1,2,0:T(8,128)(2,1)S(1)}, u32[]{:S(2)}, u32[]{:S(2)}) collective-permute-start(bf16[1,128,576]{1,2,0:T(8,128)(2,1)S(1)} %bitcast.42), channel_id=1, source_target_pairs={{0,2},{2,4},{4,6},{6,8},{8,10},{10,12},{12,14},{14,16},{16,18},{18... | collective-permute-start | bytes 442376 | tf_op jit(solution)/shard_map/ppermute | solution.py:15
  15.8 9.0 %copy-start.1 = (s32[8]{0:T(128)S(1)}, s32[8]{0:T(128)}, u32[]{:S(2)}) copy-start(s32[8]{0:T(128)} %param.9) | copy-start | bytes 100
  25.0 9.4 %collective-permute-start.2 = (bf16[2,128,576]{1,2,0:T(8,128)(2,1)S(1)}, bf16[2,128,576]{1,2,0:T(8,128)(2,1)S(1)}, u32[]{:S(2)}, u32[]{:S(2)}) collective-permute-start(bf16[2,128,576]{1,2,0:T(8,128)(2,1)S(1)} %pad_maximum_fusion.1), channel_id=1, source_target_pairs={{0,4},{2,6},{4,8},{6,10},{8,12},{10,14},{12,16},{14,18},{16,20},{1... | collective-permute-start | bytes 884744 | tf_op jit(solution)/shard_map/ppermute | solution.py:15
  34.5 16.8 %collective-permute-start.3 = (bf16[4,128,576]{1,2,0:T(8,128)(2,1)S(1)}, bf16[4,128,576]{1,2,0:T(8,128)(2,1)S(1)}, u32[]{:S(2)}, u32[]{:S(2)}) collective-permute-start(bf16[4,128,576]{1,2,0:T(8,128)(2,1)S(1)} %pad_maximum_fusion), channel_id=1, source_target_pairs={{0,8},{2,10},{4,12},{6,14},{8,16},{10,18},{12,20},{14,22},{16,24},... | collective-permute-start | bytes 1769480 | tf_op jit(solution)/shard_map/ppermute | solution.py:15
  51.5 25.6 %copy-start = (bf16[9,128,576]{1,2,0:T(8,128)(2,1)}, bf16[9,128,576]{1,2,0:T(8,128)(2,1)S(1)}, u32[]{:S(2)}) copy-start(bf16[9,128,576]{1,2,0:T(8,128)(2,1)S(1)} %constant_dynamic-update-slice_fusion) | copy-start | bytes 3981316
where the time goes:
time: 121 us
  matrix products  58.7 us (49%)
  starting transfers between devices  18.9 us (16%)
  other arithmetic  17.8 us (15%)
  waiting for transfers between devices  15.2 us (13%)
  local copies, waits for them, and re-layouts  7.68 us (6%)
  blocking collectives  2.22 us (2%)
    dot_general x1, matrix products, per_device(): jnp.einsum('thl,jkl->thjk', joined, window, preferred_element_type=jnp.fl...  25.6 us
    dot_general x1, matrix products, per_device(): jnp.einsum('thl,hlv->thv', attended, w_uv, preferred_element_type=jnp.flo...  24.1 us
    ppermute x4, starting transfers between devices, from_behind(): return lax.ppermute(x, axis, pairs)  18.9 us
    reduce_sum x1, other arithmetic, per_device(): row_total = jnp.sum(exponent, axis=(2, 3))  16.6 us
    ppermute x4, waiting for transfers between devices, from_behind(): return lax.ppermute(x, axis, pairs)  15.2 us
    dot_general x1, matrix products, per_device(): jnp.einsum('thd,hdl->thl', query_heads[:, :, :nope_width], w_uk, preferre...  9.01 us
    unnamed x9, local copies, waits for them, and re-layouts  4.55 us
    reshape x1, local copies, waits for them, and re-layouts, per_device(): projected.astype(jnp.bfloat16).reshape(tok_rows, heads_dev * value_width)  2.89 us
  transfers between devices with their start and end apart: 4, of which 2 were waited for; matrix products, arithmetic and copies ran while one was open for 12% of the time, Pallas kernels for 0%

commit v1 on v0

v1 whole, which is shorter than its diff:
```python
import functools
import math

import jax
import jax.numpy as jnp
from jax import lax
from jax.experimental import pallas as pl
from jax.experimental.pallas import tpu as pltpu
from jax.sharding import PartitionSpec as P

DOC_MOST = 1024
TAIL_MOST = 32
SUBS = 4
KEY_TILE = 256
LANES = 128
HEADS_STEP = 8

far_negative = -1e30


def order_bit(phase, core, bits):
    return 1 << ((phase + core) % bits)


def block_of_slot(slot, group_index, core, bits):
    block = group_index
    for phase in range(bits):
        if (slot >> phase) & 1:
            block = block ^ lax.shift_left(jnp.int32(1), lax.rem(jnp.int32(phase) + core, jnp.int32(bits)))
    return block


def gather_group(own, n_seq, n_heads, span):
    bits = span.bit_length() - 1
    held = own
    for phase in range(bits):
        pairs = [
            (s * n_heads + c, (s ^ order_bit(phase, c, bits)) * n_heads + c)
            for s in range(n_seq)
            for c in range(n_heads)
        ]
        got = lax.ppermute(held, ("seq", "heads"), pairs)
        held = jnp.concatenate([held, got], axis=0)
    return held


def attend(plan, info, *refs):
    (n_held, n_prev, tok, heads_step, nope, width, rank, lat, vdim, win, wpad, rows_per, span, n_docs, factor, edge) = plan
    held_refs, refs = refs[:n_held], refs[n_held:]
    prev_refs, refs = refs[:n_prev], refs[n_prev:]
    q_ref, wuk_ref, wuv_ref, o_ref, win_ref, kt_ref, j_ref, bias_ref, s0, s1, p0, p1, att_ref, sem = refs
    s_refs, p_refs = (s0, s1), (p0, p1)
    sub_tok = tok // SUBS
    rows = heads_step * sub_tok
    bits = span.bit_length() - 1
    kpad = kt_ref.shape[0]

    @pl.when(pl.program_id(0) == 0)
    def _():
        seq, core = info[0], info[1]
        place = lax.rem(seq, span)
        first = win - span * tok
        copies = []
        for turn, held in enumerate(held_refs):
            owner = lax.rem(core - turn + n_held, n_held)
            for slot in range(span):
                block = block_of_slot(slot, place, owner, bits)
                at = first + tok * lax.rem(block - place - 1 + 2 * span, span) + rows_per * owner
                at = pl.multiple_of(at, 32)
                copies.append(
                    pltpu.make_async_copy(
                        held.at[pl.ds(slot * rows_per, rows_per)], win_ref.at[pl.ds(at, rows_per)], sem.at[len(copies)]
                    )
                )
        if edge:
            lead = pltpu.make_async_copy(prev_refs[0], win_ref.at[pl.ds(0, edge)], sem.at[len(copies)])
            copies.append(lead)
        for copy in copies:
            copy.start()
        for copy in copies:
            copy.wait()
        if edge:
            at = pl.multiple_of(tok * (span - 1 - place), 32)
            copy = pltpu.make_async_copy(prev_refs[0], win_ref.at[pl.ds(at, edge)], sem.at[0])
            copy.start()
            copy.wait()
        else:
            for turn, prev in enumerate(prev_refs):
                owner = lax.rem(core - turn + n_held, n_held)
                for slot in range(span):
                    block = block_of_slot(slot, place, owner, bits)

                    @pl.when(block >= place)
                    def _():
                        at = pl.multiple_of(tok * (block - place) + rows_per * owner, 32)
                        copy = pltpu.make_async_copy(
                            prev.at[pl.ds(slot * rows_per, rows_per)], win_ref.at[pl.ds(at, rows_per)], sem.at[0]
                        )
                        copy.start()
                        copy.wait()

        for r in range(0, wpad, LANES):
            n = min(LANES, max(win - r, 0))
            if n:
                kt_ref[0:lat, r : r + n] = win_ref[r : r + n, :].T
            if n < LANES:
                kt_ref[0:lat, r + n : r + LANES] = jnp.zeros((lat, LANES - n), kt_ref.dtype)
        if kpad > lat:
            kt_ref[lat:kpad, :] = jnp.zeros((kpad - lat, wpad), kt_ref.dtype)
            j_ref[:, :, lat:kpad] = jnp.zeros((SUBS, rows, kpad - lat), j_ref.dtype)
        q_pos = seq * tok + lax.broadcasted_iota(jnp.int32, (tok, LANES), 0)
        start = jnp.zeros((tok, LANES), jnp.int32)
        end = jnp.int32(0)
        for d in range(n_docs):
            end = end + info[2 + d]
            start = jnp.where(q_pos >= end, end, start)
        for c in range(0, wpad, LANES):
            k_pos = (seq + 1) * tok - win + c + lax.broadcasted_iota(jnp.int32, (tok, LANES), 1)
            bias_ref[:, c : c + LANES] = jnp.where((k_pos >= start) & (k_pos <= q_pos), 0.0, far_negative)

    for h in range(heads_step):
        absorbed = jnp.dot(
            q_ref[:, h * width : h * width + nope], wuk_ref[h], preferred_element_type=jnp.float32
        ).astype(jnp.bfloat16)
        rope = q_ref[:, h * width + nope : (h + 1) * width]
        for g in range(SUBS):
            j_ref[g, h * sub_tok : (h + 1) * sub_tok, 0:rank] = absorbed[g * sub_tok : (g + 1) * sub_tok]
            j_ref[g, h * sub_tok : (h + 1) * sub_tok, rank:lat] = rope[g * sub_tok : (g + 1) * sub_tok]

    def reach(g):
        return win - sub_tok * (SUBS - 1 - g)

    def tiles(g):
        n = -(-reach(g) // LANES) * LANES
        return [(c, min(KEY_TILE, n - c)) for c in range(0, n, KEY_TILE)]

    def score(g):
        s_ref = s_refs[g % 2]
        top = None
        for c, w in tiles(g):
            s = jnp.dot(j_ref[g], kt_ref[:, c : c + w], preferred_element_type=jnp.float32)
            b = bias_ref[g * sub_tok : (g + 1) * sub_tok, c : c + w]
            s = (s.reshape(heads_step, sub_tok, w) + b[None]).reshape(rows, w)
            s_ref[:, c : c + w] = s
            for cc in range(0, w, LANES):
                m = s[:, cc : cc + LANES]
                top = m if top is None else jnp.maximum(top, m)
        return jnp.max(top, axis=1, keepdims=True)

    def soften(g, top):
        s_ref, p_ref = s_refs[g % 2], p_refs[g % 2]
        total = None
        for c, w in tiles(g):
            for cc in range(c, c + w, LANES):
                e = jnp.exp2((s_ref[:, cc : cc + LANES] - top) * factor)
                total = e if total is None else total + e
                p_ref[:, cc : cc + LANES] = e.astype(jnp.bfloat16)
        return jnp.sum(total, axis=1, keepdims=True)

    def mix(g, total):
        p_ref = p_refs[g % 2]
        n = reach(g)
        mixed = None
        for c in range(0, n, DOC_MOST):
            e = min(n, c + DOC_MOST)
            part = jnp.dot(p_ref[:, c:e], win_ref[c:e, 0:rank], preferred_element_type=jnp.float32)
            mixed = part if mixed is None else mixed + part
        att = (mixed * (1.0 / total)).astype(jnp.bfloat16)
        for h in range(heads_step):
            att_ref[h * tok + g * sub_tok : h * tok + (g + 1) * sub_tok, :] = att[h * sub_tok : (h + 1) * sub_tok]

    top = score(0)
    for g in range(SUBS):
        later = score(g + 1) if g + 1 < SUBS else None
        mix(g, soften(g, top))
        top = later
    for h in range(heads_step):
        o_ref[:, h * vdim : (h + 1) * vdim] = jnp.dot(
            att_ref[h * tok : (h + 1) * tok, :], wuv_ref[h], preferred_element_type=jnp.float32
        ).astype(o_ref.dtype)


def per_device(queries, latent, w_uk, w_uv, doc_lengths):
    heads_dev, nope, rank = w_uk.shape
    vdim = w_uv.shape[2]
    tok = queries.shape[0]
    width = queries.shape[1] // heads_dev
    rows_per, lat = latent.shape
    n_seq, n_heads = lax.axis_size("seq"), lax.axis_size("heads")
    span = DOC_MOST // tok
    bits = span.bit_length() - 1
    seq, core = lax.axis_index("seq"), lax.axis_index("heads")

    held = gather_group(latent, n_seq, n_heads, span)
    turned = [held]
    for turn in range(1, n_heads):
        turned.append(lax.ppermute(held, "heads", [(c, (c + turn) % n_heads) for c in range(n_heads)]))

    if n_seq == 2 * span:
        edge = TAIL_MOST
        win = DOC_MOST + edge
        place = lax.rem(seq, span)
        slot = jnp.int32(0)
        for s in range(span):
            slot = jnp.where(block_of_slot(s, place, core, bits) == span - 1, s, slot)
        edge_rows = lax.dynamic_slice_in_dim(held, (slot + 1) * rows_per - edge, edge, 0)
        prev = None
        for c in range(n_heads):
            pairs = [(s * n_heads + n_heads - 1, (s + span) * n_heads + c) for s in range(span)]
            got = lax.ppermute(edge_rows, ("seq", "heads"), pairs)
            prev = got if prev is None else jnp.where(core == c, got, prev)
        prev = [prev]
    else:
        edge = 0
        win = DOC_MOST + tok
        prev = [lax.ppermute(t, "seq", [(s, s + span) for s in range(n_seq - span)]) for t in turned]

    info = jnp.concatenate([jnp.stack([seq, core]).astype(jnp.int32), doc_lengths])
    step = min(HEADS_STEP, heads_dev)
    wpad = -(-win // KEY_TILE) * KEY_TILE
    kpad = -(-lat // LANES) * LANES
    rows = step * tok // SUBS
    plan = (
        len(turned), len(prev), tok, step, nope, width, rank, lat, vdim, win, wpad, rows_per, span,
        doc_lengths.shape[0], width**-0.5 * math.log2(math.e), edge,
    )
    hbm = pl.BlockSpec(memory_space=pl.ANY)
    return pl.pallas_call(
        functools.partial(attend, plan),
        grid=(heads_dev // step,),
        in_specs=[pl.BlockSpec(memory_space=pltpu.SMEM)]
        + [hbm] * (len(turned) + len(prev))
        + [
            pl.BlockSpec((tok, step * width), lambda i: (0, i)),
            pl.BlockSpec((step, nope, rank), lambda i: (i, 0, 0)),
            pl.BlockSpec((step, rank, vdim), lambda i: (i, 0, 0)),
        ],
        out_specs=pl.BlockSpec((tok, step * vdim), lambda i: (0, i)),
        out_shape=jax.ShapeDtypeStruct((tok, heads_dev * vdim), jnp.bfloat16),
        scratch_shapes=[
            pltpu.VMEM((win, lat), jnp.bfloat16),
            pltpu.VMEM((kpad, wpad), jnp.bfloat16),
            pltpu.VMEM((SUBS, rows, kpad), jnp.bfloat16),
            pltpu.VMEM((tok, wpad), jnp.float32),
            pltpu.VMEM((rows, wpad), jnp.float32),
            pltpu.VMEM((rows, wpad), jnp.float32),
            pltpu.VMEM((rows, wpad), jnp.bfloat16),
            pltpu.VMEM((rows, wpad), jnp.bfloat16),
            pltpu.VMEM((step * tok, rank), jnp.bfloat16),
            pltpu.SemaphoreType.DMA((span * len(turned) + 1,)),
        ],
        compiler_params=pltpu.CompilerParams(vmem_limit_bytes=32 * 1024 * 1024),
    )(info, *turned, *prev, queries, w_uk, w_uv)


def solution(mesh):
    return jax.shard_map(
        per_device,
        mesh=mesh,
        in_specs=(
            P("seq", "heads"),
            P(("seq", "heads"), None),
            P("heads", None, None),
            P("heads", None, None),
            P(),
        ),
        out_specs=P("seq", "heads"),
        check_vma=False,
    )
```

time: 121 us -> 74.8 us (0.62)
  the two profiles are of different devices: /device:TPU:0 before, /device:TPU:29 now
where the time goes in v1:
time: 74.8 us; the launch traced here: 74.3 us
  Pallas kernels  38 us (51%)
  waiting for transfers between devices  15.9 us (21%)
  local copies, waits for them, and re-layouts  10.1 us (14%)
  starting transfers between devices  7.58 us (10%)
  other arithmetic  2.57 us (3%)
    pallas_call x1, Pallas kernels, per_device(): pl.pallas_call(functools.partial(attend, plan), grid=(heads_dev // step,)...  38 us
    ppermute x3, waiting for transfers between devices, gather_group(): got = lax.ppermute(held, ('seq', 'heads'), pairs)  11.3 us
    unnamed x9, local copies, waits for them, and re-layouts  9.58 us
    ppermute x2, waiting for transfers between devices, per_device(): got = lax.ppermute(edge_rows, ('seq', 'heads'), pairs)  4.55 us
    ppermute x1, starting transfers between devices, per_device(): lax.ppermute(held, 'heads', [(c, (c + turn) % n_heads) for c in range(n_h...  3.89 us
    ppermute x2, starting transfers between devices, per_device(): got = lax.ppermute(edge_rows, ('seq', 'heads'), pairs)  1.94 us
    concatenate x2, other arithmetic, gather_group(): held = jnp.concatenate([held, got], axis=0)  1.82 us
    ppermute x3, starting transfers between devices, gather_group(): got = lax.ppermute(held, ('seq', 'heads'), pairs)  1.74 us
  transfers between devices with their start and end apart: 6, of which 4 were waited for; matrix products, arithmetic and copies ran while one was open for 2% of the time, Pallas kernels for 0%

profile of v1, /device:TPU:29, one launch (start us, length us, event | category | flops | bytes accessed | tf_op | source)
XLA Modules:
  0.0 74.3 jit_solution(6831468137322730286)
XLA Ops:
  0.0 0.2 collective-permute-start
  0.2 3.3 %collective-permute-done = bf16[64,576]{1,0:T(8,128)(2,1)S(1)} collective-permute-done((bf16[64,576]{1,0:T(8,128)(2,1)}, bf16[64,576]{1,0:T(8,128)(2,1)S(1)}, u32[]{:S(2)}, u32[]{:S(2)}) %collective-permute-start) | collective-permute-done | bytes 73760 | tf_op jit(solution)/shard_map/ppermute | solution.py:42
  3.5 0.9 %pad_maximum_fusion.1 = bf16[128,576]{1,0:T(8,128)(2,1)S(1)} fusion(bf16[64,576]{1,0:T(8,128)(2,1)S(1)} %collective-permute-done, bf16[64,576]{1,0:T(8,128)(2,1)} %param.6), kind=kLoop, calls=%fused_computation.1 | loop fusion | flops 294912 | bytes 294912 | tf_op jit(solution)/shard_map/concatenate | solution.py:43
  4.4 0.2 collective-permute-start.1
  4.6 4.0 %collective-permute-done.1 = bf16[128,576]{1,0:T(8,128)(2,1)S(1)} collective-permute-done((bf16[128,576]{1,0:T(8,128)(2,1)S(1)}, bf16[128,576]{1,0:T(8,128)(2,1)S(1)}, u32[]{:S(2)}, u32[]{:S(2)}) %collective-permute-start.1) | collective-permute-done | bytes 147488 | tf_op jit(solution)/shard_map/ppermute | solution.py:42
  8.6 0.9 %pad_maximum_fusion = bf16[256,576]{1,0:T(8,128)(2,1)S(1)} fusion(bf16[128,576]{1,0:T(8,128)(2,1)S(1)} %collective-permute-done.1, bf16[64,576]{1,0:T(8,128)(2,1)S(1)} %collective-permute-done, bf16[64,576]{1,0:T(8,128)(2,1)} %param.6), kind=kLoop, calls=%fused_computation | loop fusion | flops 884736 | bytes 589824 | tf_op jit(solution)/shard_map/concatenate | solution.py:43
  9.6 1.3 %collective-permute-start.2 = (bf16[256,576]{1,0:T(8,128)(2,1)S(1)}, bf16[256,576]{1,0:T(8,128)(2,1)S(1)}, u32[]{:S(2)}, u32[]{:S(2)}) collective-permute-start(bf16[256,576]{1,0:T(8,128)(2,1)S(1)} %pad_maximum_fusion), channel_id=1, source_target_pairs={{0,8},{1,3},{2,10},{3,1},{4,12},{5,7},{6,14},{7,5},{8,0},{9,11},{1... | collective-permute-start | bytes 884744 | tf_op jit(solution)/shard_map/ppermute | solution.py:42
  10.8 0.9 %constant_dynamic-update-slice_fusion.3 = bf16[512,576]{1,0:T(8,128)(2,1)S(1)} fusion(bf16[64,576]{1,0:T(8,128)(2,1)} %param.6), kind=kLoop, calls=%fused_computation.6 | loop fusion | bytes 155648
  11.8 4.1 %collective-permute-done.2 = bf16[256,576]{1,0:T(8,128)(2,1)S(1)} collective-permute-done((bf16[256,576]{1,0:T(8,128)(2,1)S(1)}, bf16[256,576]{1,0:T(8,128)(2,1)S(1)}, u32[]{:S(2)}, u32[]{:S(2)}) %collective-permute-start.2) | collective-permute-done | bytes 294944 | tf_op jit(solution)/shard_map/ppermute | solution.py:42
  15.9 0.2 copy.6
  16.1 3.9 %collective-permute-start.3 = (bf16[512,576]{0,1:T(8,128)(2,1)S(1)}, bf16[512,576]{0,1:T(8,128)(2,1)S(1)}, u32[]{:S(2)}, u32[]{:S(2)}) collective-permute-start(bf16[512,576]{0,1:T(8,128)(2,1)S(1)} %copy.6), channel_id=1, source_target_pairs={{0,1},{1,0},{2,3},{3,2},{4,5},{5,4},{6,7},{7,6},{8,9},{9,8},{10,11... | collective-permute-start | bytes 1769480 | tf_op jit(solution)/shard_map/ppermute | solution.py:197
  20.0 0.7 collective-permute-start.5
  20.7 1.3 %collective-permute-start.4 = (bf16[32,576]{1,0:T(8,128)(2,1)S(1)}, bf16[32,576]{1,0:T(8,128)(2,1)S(1)}, u32[]{:S(2)}, u32[]{:S(2)}) collective-permute-start(bf16[32,576]{1,0:T(8,128)(2,1)S(1)} %constant_dynamic-slice_fusion), channel_id=1, source_target_pairs={{1,17},{3,19},{5,21},{7,23},{9,25},{11,27},{13,29},{15,31}} | collective-permute-start | bytes 110600 | tf_op jit(solution)/shard_map/ppermute | solution.py:210
  22.0 0.7 pad_add_fusion.info
  22.7 0.0 collective-permute-done.5
  22.7 4.5 %collective-permute-done.4 = bf16[32,576]{1,0:T(8,128)(2,1)S(1)} collective-permute-done((bf16[32,576]{1,0:T(8,128)(2,1)S(1)}, bf16[32,576]{1,0:T(8,128)(2,1)S(1)}, u32[]{:S(2)}, u32[]{:S(2)}) %collective-permute-start.4) | collective-permute-done | bytes 36896 | tf_op jit(solution)/shard_map/ppermute | solution.py:210
  27.3 0.0 collective-permute-done.3
  27.3 0.3 copy.7.refs_1_
  27.6 0.0 copy-start
  27.6 3.4 %copy-done = bf16[64,128,512]{2,1,0:T(8,128)(2,1)S(1)} copy-done((bf16[64,128,512]{2,1,0:T(8,128)(2,1)S(1)}, bf16[64,128,512]{2,1,0:T(8,128)(2,1)}, u32[]{:S(2)}) %copy-start) | copy-done | bytes 8388632
  31.0 0.0 copy-start.1
  31.0 3.4 %copy-done.1 = bf16[64,512,128]{2,1,0:T(8,128)(2,1)S(1)} copy-done((bf16[64,512,128]{2,1,0:T(8,128)(2,1)S(1)}, bf16[64,512,128]{2,1,0:T(8,128)(2,1)}, u32[]{:S(2)}) %copy-start.1) | copy-done | bytes 8388632
  34.4 0.0 copy-start.2
  34.4 1.9 %copy-done.2 = bf16[128,12288]{1,0:T(8,128)(2,1)S(1)} copy-done((bf16[128,12288]{1,0:T(8,128)(2,1)S(1)}, bf16[128,12288]{1,0:T(8,128)(2,1)}, u32[]{:S(2)}) %copy-start.2) | copy-done | bytes 3145752
  36.3 38.0 %shard_map.55 = bf16[128,8192]{1,0:T(8,128)(2,1)} custom-call(s32[10]{0:T(128)S(1)} %pad_add_fusion.info, bf16[512,576]{1,0:T(8,128)(2,1)S(1)} %constant_dynamic-update-slice_fusion.refs_0_, bf16[512,576]{1,0:T(8,128)(2,1)S(1)} %copy.7.refs_1_, bf16[32,576]{1,0:T(8,128)(2,1)S(1)} %broadcast_select_fusion.refs_2_, bf16[128,12288]{1,0:T(8,128)(2,1)S(1)} %copy-done.2, ...), custom_call_target="tpu_custom_call" | custom-call | tf_op jit(solution)/shard_map/pallas_call | solution.py:228
  (5 shorter events, 0.1 us)
Async XLA Ops:
  0.0 3.5 %collective-permute-start = (bf16[64,576]{1,0:T(8,128)(2,1)}, bf16[64,576]{1,0:T(8,128)(2,1)S(1)}, u32[]{:S(2)}, u32[]{:S(2)}) collective-permute-start(bf16[64,576]{1,0:T(8,128)(2,1)} %param.6), channel_id=1, source_target_pairs={{0,2},{1,5},{2,0},{3,7},{4,6},{5,1},{6,4},{7,3},{8,10},{9,13},{10,... | collective-permute-start | bytes 221192 | tf_op jit(solution)/shard_map/ppermute | solution.py:42
  4.4 4.2 %collective-permute-start.1 = (bf16[128,576]{1,0:T(8,128)(2,1)S(1)}, bf16[128,576]{1,0:T(8,128)(2,1)S(1)}, u32[]{:S(2)}, u32[]{:S(2)}) collective-permute-start(bf16[128,576]{1,0:T(8,128)(2,1)S(1)} %pad_maximum_fusion.1), channel_id=1, source_target_pairs={{0,4},{1,9},{2,6},{3,11},{4,0},{5,13},{6,2},{7,15},{8,12},{9,1},{1... | collective-permute-start | bytes 442376 | tf_op jit(solution)/shard_map/ppermute | solution.py:42
  9.6 6.3 %collective-permute-start.2 = (bf16[256,576]{1,0:T(8,128)(2,1)S(1)}, bf16[256,576]{1,0:T(8,128)(2,1)S(1)}, u32[]{:S(2)}, u32[]{:S(2)}) collective-permute-start(bf16[256,576]{1,0:T(8,128)(2,1)S(1)} %pad_maximum_fusion), channel_id=1, source_target_pairs={{0,8},{1,3},{2,10},{3,1},{4,12},{5,7},{6,14},{7,5},{8,0},{9,11},{1... | collective-permute-start | bytes 884744 | tf_op jit(solution)/shard_map/ppermute | solution.py:42
  16.1 11.2 %collective-permute-start.3 = (bf16[512,576]{0,1:T(8,128)(2,1)S(1)}, bf16[512,576]{0,1:T(8,128)(2,1)S(1)}, u32[]{:S(2)}, u32[]{:S(2)}) collective-permute-start(bf16[512,576]{0,1:T(8,128)(2,1)S(1)} %copy.6), channel_id=1, source_target_pairs={{0,1},{1,0},{2,3},{3,2},{4,5},{5,4},{6,7},{7,6},{8,9},{9,8},{10,11... | collective-permute-start | bytes 1769480 | tf_op jit(solution)/shard_map/ppermute | solution.py:197
  20.0 2.7 %collective-permute-start.5 = (bf16[32,576]{1,0:T(8,128)(2,1)S(1)}, bf16[32,576]{1,0:T(8,128)(2,1)S(1)}, u32[]{:S(2)}, u32[]{:S(2)}) collective-permute-start(bf16[32,576]{1,0:T(8,128)(2,1)S(1)} %constant_dynamic-slice_fusion), channel_id=1, source_target_pairs={{1,16},{3,18},{5,20},{7,22},{9,24},{11,26},{13,28},{15,30}} | collective-permute-start | bytes 110600 | tf_op jit(solution)/shard_map/ppermute | solution.py:210
  20.7 6.6 %collective-permute-start.4 = (bf16[32,576]{1,0:T(8,128)(2,1)S(1)}, bf16[32,576]{1,0:T(8,128)(2,1)S(1)}, u32[]{:S(2)}, u32[]{:S(2)}) collective-permute-start(bf16[32,576]{1,0:T(8,128)(2,1)S(1)} %constant_dynamic-slice_fusion), channel_id=1, source_target_pairs={{1,17},{3,19},{5,21},{7,23},{9,25},{11,27},{13,29},{15,31}} | collective-permute-start | bytes 110600 | tf_op jit(solution)/shard_map/ppermute | solution.py:210
  27.6 3.4 %copy-start = (bf16[64,128,512]{2,1,0:T(8,128)(2,1)S(1)}, bf16[64,128,512]{2,1,0:T(8,128)(2,1)}, u32[]{:S(2)}) copy-start(bf16[64,128,512]{2,1,0:T(8,128)(2,1)} %refs_4_.1) | copy-start | bytes 25165828
  31.0 3.4 %copy-start.1 = (bf16[64,512,128]{2,1,0:T(8,128)(2,1)S(1)}, bf16[64,512,128]{2,1,0:T(8,128)(2,1)}, u32[]{:S(2)}) copy-start(bf16[64,512,128]{2,1,0:T(8,128)(2,1)} %refs_5_.1) | copy-start | bytes 25165828
  34.4 1.9 %copy-start.2 = (bf16[128,12288]{1,0:T(8,128)(2,1)S(1)}, bf16[128,12288]{1,0:T(8,128)(2,1)}, u32[]{:S(2)}) copy-start(bf16[128,12288]{1,0:T(8,128)(2,1)} %refs_3_.1) | copy-start | bytes 9437188

commit v2 on v0

v2 whole, which is shorter than its diff:
```python
import functools
import math

import jax
import jax.numpy as jnp
from jax import lax
from jax.experimental import pallas as pl
from jax.experimental.pallas import tpu as pltpu
from jax.sharding import PartitionSpec as P

DOC_MOST = 1024
TAIL_MOST = 32
SUBS = 4
KEY_TILE = 256
LANES = 128
HEADS_GROUP = 8
HEADS_STEP = 16

far_negative = -1e30


def absorb(tok, nope, width, rank, lat, q_ref, wuk_ref, wuv_hbm, j_ref, wuv_ref, sem):
    step = pl.program_id(0)
    sub_tok = tok // SUBS
    rows = j_ref.shape[2]
    group = rows // sub_tok
    groups_step = wuk_ref.shape[0] // group
    kpad = j_ref.shape[3]
    copy = pltpu.make_async_copy(wuv_hbm, wuv_ref, sem)

    @pl.when(step == 0)
    def _():
        copy.start()

    for h in range(wuk_ref.shape[0]):
        absorbed = jnp.dot(
            q_ref[:, h * width : h * width + nope], wuk_ref[h], preferred_element_type=jnp.float32
        ).astype(jnp.bfloat16)
        rope = q_ref[:, h * width + nope : (h + 1) * width]
        if kpad > lat:
            rope = jnp.concatenate([rope, jnp.zeros((tok, kpad - lat), rope.dtype)], axis=1)
        i = step * groups_step + h // group
        at = (h % group) * sub_tok
        for g in range(SUBS):
            j_ref[i, g, at : at + sub_tok, 0:rank] = absorbed[g * sub_tok : (g + 1) * sub_tok]
            j_ref[i, g, at : at + sub_tok, rank:kpad] = rope[g * sub_tok : (g + 1) * sub_tok]

    @pl.when(step == pl.num_programs(0) - 1)
    def _():
        copy.wait()


def attend(plan, info, *refs):
    (n_heads, tok, rank, lat, vdim, win, wpad, span, n_docs, factor) = plan
    per = -(-span // n_heads)
    own, refs = refs[0], refs[1:]
    pieces, refs = refs[: per * n_heads], refs[per * n_heads :]
    j_ref, wuv_ref, o_ref, win_ref, kt_ref, bias_ref, s0, s1, p0, p1, att_ref = refs
    s_refs, p_refs = (s0, s1), (p0, p1)
    sub_tok = tok // SUBS
    n_groups, _, rows, kpad = j_ref.shape
    group = rows // sub_tok

    seq, core = info[0], info[1]
    lead = win - span * tok
    win_ref[win - tok : win, :] = own[...]
    for turn in range(n_heads):
        owner = lax.rem(core - turn + n_heads, n_heads)
        for n in range(per):
            piece = pieces[turn * per + n]
            shift = 1 + owner * per + n
            if lead == tok:
                at = tok * (span - shift)
                win_ref[pl.ds(pl.multiple_of(at, tok), tok), :] = piece[...]
            else:
                at = jnp.maximum(lead + tok * (span - 1 - shift), 0)
                is_last = shift == span
                part = jnp.where(is_last, piece[tok - lead : tok, :], piece[0:lead, :])
                win_ref[pl.ds(pl.multiple_of(at, lead), lead), :] = part
                at = jnp.where(is_last, win, at + lead)
                win_ref[pl.ds(pl.multiple_of(at, lead), tok - lead), :] = piece[lead:tok, :]
    q_pos = seq * tok + lax.broadcasted_iota(jnp.int32, (tok, LANES), 0)
    start = jnp.zeros((tok, LANES), jnp.int32)
    end = jnp.int32(0)
    for d in range(n_docs):
        end = end + info[2 + d]
        start = jnp.where(q_pos >= end, end, start)
    for c in range(0, wpad, LANES):
        k_pos = (seq + 1) * tok - win + c + lax.broadcasted_iota(jnp.int32, (tok, LANES), 1)
        bias_ref[:, c : c + LANES] = jnp.where((k_pos >= start) & (k_pos <= q_pos), 0.0, far_negative)

    for r in range(0, wpad, LANES):
        n = min(LANES, max(win - r, 0))
        if n:
            kt_ref[0:lat, r : r + n] = win_ref[r : r + n, :].T
        if n < LANES:
            kt_ref[0:lat, r + n : r + LANES] = jnp.zeros((lat, LANES - n), kt_ref.dtype)
    if kpad > lat:
        kt_ref[lat:kpad, :] = jnp.zeros((kpad - lat, wpad), kt_ref.dtype)

    def reach(g):
        return win - sub_tok * (SUBS - 1 - g)

    def tiles(g):
        n = -(-reach(g) // LANES) * LANES
        return [(c, min(KEY_TILE, n - c)) for c in range(0, n, KEY_TILE)]

    def score(i, g):
        s_ref = s_refs[g % 2]
        top = None
        for c, w in tiles(g):
            s = jnp.dot(j_ref[i, g], kt_ref[:, c : c + w], preferred_element_type=jnp.float32)
            b = bias_ref[g * sub_tok : (g + 1) * sub_tok, c : c + w]
            s = (s.reshape(group, sub_tok, w) + b[None]).reshape(rows, w)
            s_ref[:, c : c + w] = s
            for cc in range(0, w, LANES):
                m = s[:, cc : cc + LANES]
                top = m if top is None else jnp.maximum(top, m)
        return jnp.max(top, axis=1, keepdims=True)

    def soften(g, top):
        s_ref, p_ref = s_refs[g % 2], p_refs[g % 2]
        total = None
        for c, w in tiles(g):
            for cc in range(c, c + w, LANES):
                e = jnp.exp2((s_ref[:, cc : cc + LANES] - top) * factor)
                total = e if total is None else total + e
                p_ref[:, cc : cc + LANES] = e.astype(jnp.bfloat16)
        return jnp.sum(total, axis=1, keepdims=True)

    def mix(g, total):
        p_ref = p_refs[g % 2]
        n = reach(g)
        mixed = None
        for c in range(0, n, DOC_MOST):
            e = min(n, c + DOC_MOST)
            part = jnp.dot(p_ref[:, c:e], win_ref[c:e, 0:rank], preferred_element_type=jnp.float32)
            mixed = part if mixed is None else mixed + part
        att = (mixed * (1.0 / total)).astype(jnp.bfloat16)
        for h in range(group):
            att_ref[h * tok + g * sub_tok : h * tok + (g + 1) * sub_tok, :] = att[h * sub_tok : (h + 1) * sub_tok]

    def one_group(i, top):
        for g in range(SUBS):
            if g + 1 < SUBS:
                later = score(i, g + 1)
            else:
                later = score(jnp.minimum(i + 1, n_groups - 1), 0)
            mix(g, soften(g, top))
            top = later
        for h in range(group):
            out = jnp.dot(
                att_ref[h * tok : (h + 1) * tok, :], wuv_ref[i * group + h], preferred_element_type=jnp.float32
            ).astype(o_ref.dtype)
            at = pl.multiple_of((i * group + h) * vdim, vdim)
            o_ref[:, pl.ds(at, vdim)] = out
        return top

    lax.fori_loop(0, n_groups, one_group, score(0, 0))


def near(arrays):
    return [pltpu.with_memory_space_constraint(x, pltpu.VMEM) for x in arrays]


def far(arrays):
    return [pltpu.with_memory_space_constraint(x, pltpu.HBM) for x in arrays]


def per_device(queries, latent, w_uk, w_uv, doc_lengths):
    heads_dev, nope, rank = w_uk.shape
    vdim = w_uv.shape[2]
    tok = queries.shape[0]
    width = queries.shape[1] // heads_dev
    rows_per, lat = latent.shape
    n_seq, n_heads = lax.axis_size("seq"), lax.axis_size("heads")
    span = DOC_MOST // tok
    seq, core = lax.axis_index("seq"), lax.axis_index("heads")
    group = min(HEADS_GROUP, heads_dev)
    step = min(HEADS_STEP, heads_dev)
    rows = group * tok // SUBS
    kpad = -(-lat // LANES) * LANES

    per = -(-span // n_heads)
    far_block = n_seq - span - 1

    def asked(source, target):
        return source >= 0 and (target < n_seq - span or source >= far_block)

    win = DOC_MOST + (TAIL_MOST if n_seq == 2 * span else tok)
    own = lax.all_gather(latent, "heads", axis=0, tiled=True)
    info = jnp.concatenate([jnp.stack([seq, core]).astype(jnp.int32), doc_lengths])
    direct = []
    for n in range(per):
        pairs = []
        for c in range(n_heads):
            shift = 1 + c * per + n
            if shift <= span:
                pairs += [
                    ((t - shift) * n_heads + c, t * n_heads + c) for t in range(n_seq) if asked(t - shift, t)
                ]
        direct.append(lax.ppermute(own, ("seq", "heads"), pairs))
    own, info, queries = lax.optimization_barrier((own, info, queries))

    hbm = pl.BlockSpec(memory_space=pl.ANY)
    vmem = pl.BlockSpec(memory_space=pltpu.VMEM)
    j_shape = (heads_dev // group, SUBS, rows, kpad)
    joined, w_uv_near = pl.pallas_call(
        functools.partial(absorb, tok, nope, width, rank, lat),
        grid=(heads_dev // step,),
        in_specs=[
            pl.BlockSpec((tok, step * width), lambda i: (0, i)),
            pl.BlockSpec((step, nope, rank), lambda i: (i, 0, 0)),
            hbm,
        ],
        out_specs=[vmem, vmem],
        out_shape=[pltpu.VMEM(j_shape, jnp.bfloat16), pltpu.VMEM(w_uv.shape, w_uv.dtype)],
        scratch_shapes=[pltpu.SemaphoreType.DMA],
        compiler_params=pltpu.CompilerParams(vmem_limit_bytes=24 * 1024 * 1024),
        cost_estimate=pl.CostEstimate(
            flops=2 * tok * heads_dev * nope * rank, bytes_accessed=2 * (w_uk.size + w_uv.size + queries.size), transcendentals=0
        ),
    )(*far([queries, w_uk, w_uv]))
    direct, joined, w_uv_near = lax.optimization_barrier((direct, joined, w_uv_near))

    pieces = list(direct)
    for turn in range(1, n_heads):
        pairs = [(c, (c + turn) % n_heads) for c in range(n_heads)]
        pieces += [lax.ppermute(x, "heads", pairs) for x in direct]

    wpad = -(-win // KEY_TILE) * KEY_TILE
    plan = (
        n_heads, tok, rank, lat, vdim, win, wpad, span, doc_lengths.shape[0], width**-0.5 * math.log2(math.e),
    )
    return pl.pallas_call(
        functools.partial(attend, plan),
        in_specs=[pl.BlockSpec(memory_space=pltpu.SMEM)] + [vmem] * (len(pieces) + 3),
        out_specs=vmem,
        out_shape=jax.ShapeDtypeStruct((tok, heads_dev * vdim), jnp.bfloat16),
        scratch_shapes=[
            pltpu.VMEM((win + tok, lat), jnp.bfloat16),
            pltpu.VMEM((kpad, wpad), jnp.bfloat16),
            pltpu.VMEM((tok, wpad), jnp.float32),
            pltpu.VMEM((rows, wpad), jnp.float32),
            pltpu.VMEM((rows, wpad), jnp.float32),
            pltpu.VMEM((rows, wpad), jnp.bfloat16),
            pltpu.VMEM((rows, wpad), jnp.bfloat16),
            pltpu.VMEM((group * tok, rank), jnp.bfloat16),
        ],
        compiler_params=pltpu.CompilerParams(vmem_limit_bytes=24 * 1024 * 1024),
    )(info, *near([own, *pieces, joined, w_uv_near]))


def solution(mesh):
    return jax.shard_map(
        per_device,
        mesh=mesh,
        in_specs=(
            P("seq", "heads"),
            P(("seq", "heads"), None),
            P("heads", None, None),
            P("heads", None, None),
            P(),
        ),
        out_specs=P("seq", "heads"),
        check_vma=False,
    )
```

time: 121 us -> 61.3 us (0.51)
  the two profiles are of different devices: /device:TPU:0 before, /device:TPU:3 now
where the time goes in v2:
time: 61.3 us; the launch traced here: 61 us
  Pallas kernels  40.8 us (67%)
  starting transfers between devices  15.7 us (26%)
  blocking collectives  2.44 us (4%)
  waiting for transfers between devices  1.33 us (2%)
  other arithmetic  0.73 us (1%)
    pallas_call x1, Pallas kernels, per_device(): pl.pallas_call(functools.partial(attend, plan), in_specs=[pl.BlockSpec(me...  32.8 us
    ppermute x4, starting transfers between devices, per_device(): direct.append(lax.ppermute(own, ('seq', 'heads'), pairs))  11.6 us
    pallas_call x1, Pallas kernels, per_device(): pl.pallas_call(functools.partial(absorb, tok, nope, width, rank, lat), gr...  7.96 us
    ppermute x4, starting transfers between devices, per_device(): pieces += [lax.ppermute(x, 'heads', pairs) for x in direct]  4.07 us
    all_gather x1, blocking collectives, per_device(): own = lax.all_gather(latent, 'heads', axis=0, tiled=True)  2.44 us
    ppermute x4, waiting for transfers between devices, per_device(): pieces += [lax.ppermute(x, 'heads', pairs) for x in direct]  1.31 us
  transfers between devices with their start and end apart: 8, of which 4 were waited for; matrix products, arithmetic and copies ran while one was open for 1% of the time, Pallas kernels for 13%

profile of v2, /device:TPU:3, one launch (start us, length us, event | category | flops | bytes accessed | tf_op | source)
XLA Modules:
  0.0 61.0 jit_solution(7695351753042720525)
XLA Ops:
  0.0 2.4 %all_gather.3.refs_0_ = bf16[128,576]{1,0:T(8,128)(2,1)S(1)} all-gather(bf16[64,576]{1,0:T(8,128)(2,1)} %param.6), channel_id=1, replica_groups=mesh['seq'=16,'heads'=2] {'heads'}, dimensions={0}, use_global_device_ids=true | all-gather | bytes 221184 | tf_op jit(solution)/shard_map/all_gather | solution.py:191
  2.4 0.7 %collective-permute-start.3 = (bf16[128,576]{1,0:T(8,128)(2,1)S(1)}, bf16[128,576]{1,0:T(8,128)(2,1)S(1)}, u32[]{:S(2)}, u32[]{:S(2)}) collective-permute-start(bf16[128,576]{1,0:T(8,128)(2,1)S(1)} %all_gather.3.refs_0_), channel_id=1, source_target_pairs={{0,8},{2,10},{4,12},{6,14},{14,22},{16,24},{18,26},{20,28},{22,30}... | collective-permute-start | bytes 442376 | tf_op jit(solution)/shard_map/ppermute | solution.py:202
  3.1 0.7 %collective-permute-start.2 = (bf16[128,576]{1,0:T(8,128)(2,1)S(1)}, bf16[128,576]{1,0:T(8,128)(2,1)S(1)}, u32[]{:S(2)}, u32[]{:S(2)}) collective-permute-start(bf16[128,576]{1,0:T(8,128)(2,1)S(1)} %all_gather.3.refs_0_), channel_id=1, source_target_pairs={{0,6},{2,8},{4,10},{6,12},{8,14},{14,20},{16,22},{18,24},{20,26},{... | collective-permute-start | bytes 442376 | tf_op jit(solution)/shard_map/ppermute | solution.py:202
  3.8 9.0 %collective-permute-start.1 = (bf16[128,576]{1,0:T(8,128)(2,1)S(1)}, bf16[128,576]{1,0:T(8,128)(2,1)S(1)}, u32[]{:S(2)}, u32[]{:S(2)}) collective-permute-start(bf16[128,576]{1,0:T(8,128)(2,1)S(1)} %all_gather.3.refs_0_), channel_id=1, source_target_pairs={{0,4},{2,6},{4,8},{6,10},{8,12},{10,14},{14,18},{16,20},{18,22},{2... | collective-permute-start | bytes 442376 | tf_op jit(solution)/shard_map/ppermute | solution.py:202
  12.8 1.3 %collective-permute-start = (bf16[128,576]{1,0:T(8,128)(2,1)S(1)}, bf16[128,576]{1,0:T(8,128)(2,1)S(1)}, u32[]{:S(2)}, u32[]{:S(2)}) collective-permute-start(bf16[128,576]{1,0:T(8,128)(2,1)S(1)} %all_gather.3.refs_0_), channel_id=1, source_target_pairs={{0,2},{2,4},{4,6},{6,8},{8,10},{10,12},{12,14},{14,16},{16,18},{18... | collective-permute-start | bytes 442376 | tf_op jit(solution)/shard_map/ppermute | solution.py:202
  14.1 0.7 %pad_add_fusion.info = s32[10]{0:T(128)S(1)} fusion(s32[8]{0:T(128)} %param.9, s32[1]{0:T(128)} %bitcast.1, s32[1]{0:T(128)} %bitcast), kind=kLoop, calls=%fused_computation | loop fusion | flops 20 | bytes 80 | tf_op jit(solution)/shard_map/concatenate | solution.py:192
  14.8 8.0 %shard_map.55 = (bf16[8,4,256,640]{3,2,1,0:T(8,128)(2,1)S(1)}, bf16[64,512,128]{2,1,0:T(8,128)(2,1)S(1)}) custom-call(bf16[128,12288]{1,0:T(8,128)(2,1)} %q_ref, bf16[64,128,512]{2,1,0:T(8,128)(2,1)} %wuk_ref.1, bf16[64,512,128]{2,1,0:T(8,128)(2,1)} %wuv_hbm.1), custom_call_target="tpu_custom_call" | custom-call | flops 1073741824 | bytes 19922944 | tf_op jit(solution)/shard_map/pallas_call | solution.py:208
  22.8 0.0 collective-permute-done.3.refs_4_
  22.8 0.0 collective-permute-done.2.refs_3_
  22.8 0.0 collective-permute-done.1.refs_2_
  22.8 0.0 collective-permute-done.refs_1_
  22.8 3.5 %collective-permute-start.4 = (bf16[128,576]{1,0:T(8,128)(2,1)S(1)}, bf16[128,576]{1,0:T(8,128)(2,1)S(1)}, u32[]{:S(2)}, u32[]{:S(2)}) collective-permute-start(bf16[128,576]{1,0:T(8,128)(2,1)S(1)} %collective-permute-done.refs_1_), channel_id=1, source_target_pairs={{0,1},{1,0},{2,3},{3,2},{4,5},{5,4},{6,7},{7,6},{8,9},{9,8},{10,11... | collective-permute-start | bytes 442376 | tf_op jit(solution)/shard_map/ppermute | solution.py:229
  26.3 0.1 collective-permute-start.5
  26.4 0.4 collective-permute-start.6
  26.8 0.1 collective-permute-start.7
  26.9 0.4 collective-permute-done.4.refs_5_
  27.3 0.4 collective-permute-done.5.refs_6_
  27.7 0.2 collective-permute-done.6.refs_7_
  27.9 0.3 collective-permute-done.7.refs_8_
  28.2 32.8 %shard_map.56 = bf16[128,8192]{1,0:T(8,128)(2,1)} custom-call(s32[10]{0:T(128)S(1)} %pad_add_fusion.info, bf16[128,576]{1,0:T(8,128)(2,1)S(1)} %all_gather.3.refs_0_, bf16[128,576]{1,0:T(8,128)(2,1)S(1)} %collective-permute-done.refs_1_, bf16[128,576]{1,0:T(8,128)(2,1)S(1)} %collective-permute-done.1.refs_2_, ...), custom_call_target="tpu_custom_call" | custom-call | tf_op jit(solution)/shard_map/pallas_call | solution.py:235
Async XLA Ops:
  2.4 20.3 %collective-permute-start.3 = (bf16[128,576]{1,0:T(8,128)(2,1)S(1)}, bf16[128,576]{1,0:T(8,128)(2,1)S(1)}, u32[]{:S(2)}, u32[]{:S(2)}) collective-permute-start(bf16[128,576]{1,0:T(8,128)(2,1)S(1)} %all_gather.3.refs_0_), channel_id=1, source_target_pairs={{0,8},{2,10},{4,12},{6,14},{14,22},{16,24},{18,26},{20,28},{22,30}... | collective-permute-start | bytes 442376 | tf_op jit(solution)/shard_map/ppermute | solution.py:202
  3.1 19.7 %collective-permute-start.2 = (bf16[128,576]{1,0:T(8,128)(2,1)S(1)}, bf16[128,576]{1,0:T(8,128)(2,1)S(1)}, u32[]{:S(2)}, u32[]{:S(2)}) collective-permute-start(bf16[128,576]{1,0:T(8,128)(2,1)S(1)} %all_gather.3.refs_0_), channel_id=1, source_target_pairs={{0,6},{2,8},{4,10},{6,12},{8,14},{14,20},{16,22},{18,24},{20,26},{... | collective-permute-start | bytes 442376 | tf_op jit(solution)/shard_map/ppermute | solution.py:202
  3.8 19.0 %collective-permute-start.1 = (bf16[128,576]{1,0:T(8,128)(2,1)S(1)}, bf16[128,576]{1,0:T(8,128)(2,1)S(1)}, u32[]{:S(2)}, u32[]{:S(2)}) collective-permute-start(bf16[128,576]{1,0:T(8,128)(2,1)S(1)} %all_gather.3.refs_0_), channel_id=1, source_target_pairs={{0,4},{2,6},{4,8},{6,10},{8,12},{10,14},{14,18},{16,20},{18,22},{2... | collective-permute-start | bytes 442376 | tf_op jit(solution)/shard_map/ppermute | solution.py:202
  12.8 10.1 %collective-permute-start = (bf16[128,576]{1,0:T(8,128)(2,1)S(1)}, bf16[128,576]{1,0:T(8,128)(2,1)S(1)}, u32[]{:S(2)}, u32[]{:S(2)}) collective-permute-start(bf16[128,576]{1,0:T(8,128)(2,1)S(1)} %all_gather.3.refs_0_), channel_id=1, source_target_pairs={{0,2},{2,4},{4,6},{6,8},{8,10},{10,12},{12,14},{14,16},{16,18},{18... | collective-permute-start | bytes 442376 | tf_op jit(solution)/shard_map/ppermute | solution.py:202
  22.8 4.5 %collective-permute-start.4 = (bf16[128,576]{1,0:T(8,128)(2,1)S(1)}, bf16[128,576]{1,0:T(8,128)(2,1)S(1)}, u32[]{:S(2)}, u32[]{:S(2)}) collective-permute-start(bf16[128,576]{1,0:T(8,128)(2,1)S(1)} %collective-permute-done.refs_1_), channel_id=1, source_target_pairs={{0,1},{1,0},{2,3},{3,2},{4,5},{5,4},{6,7},{7,6},{8,9},{9,8},{10,11... | collective-permute-start | bytes 442376 | tf_op jit(solution)/shard_map/ppermute | solution.py:229
  26.3 1.4 %collective-permute-start.5 = (bf16[128,576]{1,0:T(8,128)(2,1)S(1)}, bf16[128,576]{1,0:T(8,128)(2,1)S(1)}, u32[]{:S(2)}, u32[]{:S(2)}) collective-permute-start(bf16[128,576]{1,0:T(8,128)(2,1)S(1)} %collective-permute-done.1.refs_2_), channel_id=1, source_target_pairs={{0,1},{1,0},{2,3},{3,2},{4,5},{5,4},{6,7},{7,6},{8,9},{9,8},{10,11... | collective-permute-start | bytes 442376 | tf_op jit(solution)/shard_map/ppermute | solution.py:229
  26.4 1.6 %collective-permute-start.6 = (bf16[128,576]{1,0:T(8,128)(2,1)S(1)}, bf16[128,576]{1,0:T(8,128)(2,1)S(1)}, u32[]{:S(2)}, u32[]{:S(2)}) collective-permute-start(bf16[128,576]{1,0:T(8,128)(2,1)S(1)} %collective-permute-done.2.refs_3_), channel_id=1, source_target_pairs={{0,1},{1,0},{2,3},{3,2},{4,5},{5,4},{6,7},{7,6},{8,9},{9,8},{10,11... | collective-permute-start | bytes 442376 | tf_op jit(solution)/shard_map/ppermute | solution.py:229
  26.8 1.4 %collective-permute-start.7 = (bf16[128,576]{1,0:T(8,128)(2,1)S(1)}, bf16[128,576]{1,0:T(8,128)(2,1)S(1)}, u32[]{:S(2)}, u32[]{:S(2)}) collective-permute-start(bf16[128,576]{1,0:T(8,128)(2,1)S(1)} %collective-permute-done.3.refs_4_), channel_id=1, source_target_pairs={{0,1},{1,0},{2,3},{3,2},{4,5},{5,4},{6,7},{7,6},{8,9},{9,8},{10,11... | collective-permute-start | bytes 442376 | tf_op jit(solution)/shard_map/ppermute | solution.py:229

commit v3 on v2

v3 whole, which is shorter than its diff:
```python
import functools
import math

import jax
import jax.numpy as jnp
from jax import lax
from jax.experimental import pallas as pl
from jax.experimental.pallas import tpu as pltpu
from jax.sharding import PartitionSpec as P

DOC_MOST = 1024
TAIL_MOST = 32
SUBS = 4
KEY_TILE = 256
LANES = 128
HEADS_GROUP = 8
HEADS_STEP = 16
PARTS = (1, 3)
LIGHT_TILES = 2

far_negative = -1e30


def absorb(tok, nope, width, rank, lat, base, first, brings, *refs):
    step = pl.program_id(0)
    q_ref, wuk_ref, refs = refs[0], refs[1], refs[2:]
    if not first:
        refs = refs[1:]
    if brings:
        wuv_hbm, j_ref, wuv_ref, sem = refs
        copy = pltpu.make_async_copy(wuv_hbm, wuv_ref, sem)

        @pl.when(step == 0)
        def _():
            copy.start()
    else:
        (j_ref,) = refs
    sub_tok = tok // SUBS
    rows = j_ref.shape[2]
    group = rows // sub_tok
    groups_step = wuk_ref.shape[0] // group
    kpad = j_ref.shape[3]

    for h in range(wuk_ref.shape[0]):
        absorbed = jnp.dot(
            q_ref[:, h * width : h * width + nope], wuk_ref[h], preferred_element_type=jnp.float32
        ).astype(jnp.bfloat16)
        rope = q_ref[:, h * width + nope : (h + 1) * width]
        if kpad > lat:
            rope = jnp.concatenate([rope, jnp.zeros((tok, kpad - lat), rope.dtype)], axis=1)
        i = (base + step) * groups_step + h // group
        at = (h % group) * sub_tok
        for g in range(SUBS):
            j_ref[i, g, at : at + sub_tok, 0:rank] = absorbed[g * sub_tok : (g + 1) * sub_tok]
            j_ref[i, g, at : at + sub_tok, rank:kpad] = rope[g * sub_tok : (g + 1) * sub_tok]

    if brings:

        @pl.when(step == pl.num_programs(0) - 1)
        def _():
            copy.wait()


def pack(n_heads, edge, *refs):
    o_ref = refs[-1]
    core = lax.axis_index("heads")
    rows_per = refs[0].shape[0]
    for turn in range(n_heads):
        owner = lax.rem(core - turn + n_heads, n_heads)
        o_ref[pl.ds(pl.multiple_of(rows_per * owner, rows_per), rows_per), :] = refs[turn][...]
    if edge:
        rows = refs[n_heads][rows_per - edge :, :]
        for c in range(1, n_heads):
            rows = jnp.where(core == c, refs[n_heads + c][rows_per - edge :, :], rows)
        o_ref[rows_per * n_heads :, :] = rows


def partners(span, n_heads):
    ks = sorted(range(1, span), key=lambda k: (k.bit_count(), k))
    per = -(-len(ks) // n_heads)
    ks += [0] * (per * n_heads - len(ks))
    return [ks[n * n_heads : (n + 1) * n_heads] for n in range(per)]


def attend(plan, lengths, *refs):
    (n_heads, tok, rank, lat, vdim, win, wpad, span, n_docs, factor, edge) = plan
    per = -(-(span - 1 if edge else span) // n_heads)
    own, refs = refs[0], refs[1:]
    pieces, refs = refs[: per * n_heads], refs[per * n_heads :]
    j_ref, wuv_ref, o_ref, win_ref, kt_ref, bias_ref, s0, s1, p0, p1, att_ref = refs
    s_refs, p_refs = (s0, s1), (p0, p1)
    sub_tok = tok // SUBS
    n_groups, _, rows, kpad = j_ref.shape
    group = rows // sub_tok

    seq, core = lax.axis_index("seq"), lax.axis_index("heads")
    if edge:
        place = lax.rem(seq, span)
        held = [(own, place, place)]
        for turn in range(n_heads):
            owner = lax.rem(core - turn + n_heads, n_heads)
            for n, ks in enumerate(partners(span, n_heads)):
                k = jnp.int32(0)
                for c, kc in enumerate(ks):
                    k = jnp.where(owner == c, kc, k)
                block = lax.bitwise_xor(place, k)
                held.append((pieces[turn * per + n], block, jnp.where(k == 0, span, block)))
        for piece, block, _ in held[1:] + held[:1]:
            at = edge + tok * lax.rem(block - place - 1 + 2 * span, span)
            win_ref[pl.ds(pl.multiple_of(at, edge), tok), :] = piece[0:tok, :]
        win_ref[0:edge, :] = own[0:edge, :]
        for piece, _, block in held:
            at = jnp.where(block == span // 2 - 1, tok * (span - 1 - place), win)
            win_ref[pl.ds(pl.multiple_of(at, edge), edge), :] = piece[tok : tok + edge, :]
    else:
        win_ref[win - tok : win, :] = own[...]
        for turn in range(n_heads):
            owner = lax.rem(core - turn + n_heads, n_heads)
            for n in range(per):
                at = tok * (span - 1 - owner * per - n)
                win_ref[pl.ds(pl.multiple_of(at, tok), tok), :] = pieces[turn * per + n][...]
    q_pos = seq * tok + lax.broadcasted_iota(jnp.int32, (tok, LANES), 0)
    start = jnp.zeros((tok, LANES), jnp.int32)
    end = jnp.int32(0)
    for d in range(n_docs):
        end = end + lengths[d]
        start = jnp.where(q_pos >= end, end, start)
    for c in range(0, wpad, LANES):
        k_pos = (seq + 1) * tok - win + c + lax.broadcasted_iota(jnp.int32, (tok, LANES), 1)
        bias_ref[:, c : c + LANES] = jnp.where((k_pos >= start) & (k_pos <= q_pos), 0.0, far_negative)

    for r in range(0, wpad, LANES):
        n = min(LANES, max(win - r, 0))
        if n:
            kt_ref[0:lat, r : r + n] = win_ref[r : r + n, :].T
        if n < LANES:
            kt_ref[0:lat, r + n : r + LANES] = jnp.zeros((lat, LANES - n), kt_ref.dtype)
    if kpad > lat:
        kt_ref[lat:kpad, :] = jnp.zeros((kpad - lat, wpad), kt_ref.dtype)

    def groups_from(skip):
        def reach(g):
            return win - sub_tok * (SUBS - 1 - g)

        def tiles(g):
            n = -(-reach(g) // LANES) * LANES
            return [(c, min(KEY_TILE, n - c)) for c in range(skip, n, KEY_TILE)]

        def score(i, g):
            s_ref = s_refs[g % 2]
            top = None
            for c, w in tiles(g):
                s = jnp.dot(j_ref[i, g], kt_ref[:, c : c + w], preferred_element_type=jnp.float32)
                b = bias_ref[g * sub_tok : (g + 1) * sub_tok, c : c + w]
                s = (s.reshape(group, sub_tok, w) + b[None]).reshape(rows, w)
                s_ref[:, c : c + w] = s
                for cc in range(0, w, LANES):
                    m = s[:, cc : cc + LANES]
                    top = m if top is None else jnp.maximum(top, m)
            return jnp.max(top, axis=1, keepdims=True)

        def soften(g, top):
            s_ref, p_ref = s_refs[g % 2], p_refs[g % 2]
            total = None
            for c, w in tiles(g):
                for cc in range(c, c + w, LANES):
                    e = jnp.exp2((s_ref[:, cc : cc + LANES] - top) * factor)
                    total = e if total is None else total + e
                    p_ref[:, cc : cc + LANES] = e.astype(jnp.bfloat16)
            return jnp.sum(total, axis=1, keepdims=True)

        def mix(g, total):
            p_ref = p_refs[g % 2]
            n = reach(g)
            mixed = None
            for c in range(skip, n, DOC_MOST - skip):
                e = min(n, c + DOC_MOST - skip)
                part = jnp.dot(p_ref[:, c:e], win_ref[c:e, 0:rank], preferred_element_type=jnp.float32)
                mixed = part if mixed is None else mixed + part
            att = (mixed * (1.0 / total)).astype(jnp.bfloat16)
            for h in range(group):
                att_ref[h * tok + g * sub_tok : h * tok + (g + 1) * sub_tok, :] = att[h * sub_tok : (h + 1) * sub_tok]

        def one_group(i, top):
            for g in range(SUBS):
                if g + 1 < SUBS:
                    later = score(i, g + 1)
                else:
                    later = score(jnp.minimum(i + 1, n_groups - 1), 0)
                mix(g, soften(g, top))
                top = later
            for h in range(group):
                out = jnp.dot(
                    att_ref[h * tok : (h + 1) * tok, :], wuv_ref[i * group + h], preferred_element_type=jnp.float32
                ).astype(o_ref.dtype)
                at = pl.multiple_of((i * group + h) * vdim, vdim)
                o_ref[:, pl.ds(at, vdim)] = out
            return top

        lax.fori_loop(0, n_groups, one_group, score(0, 0))

    block_start, end = jnp.int32(0), jnp.int32(0)
    for d in range(n_docs):
        end = end + lengths[d]
        block_start = jnp.where(seq * tok >= end, end, block_start)
    low = block_start - ((seq + 1) * tok - win)
    for tiles_out in range(LIGHT_TILES + 1):
        least = low >= tiles_out * KEY_TILE
        most = low < (tiles_out + 1) * KEY_TILE
        if tiles_out == 0:
            taken = most
        elif tiles_out == LIGHT_TILES:
            taken = least
        else:
            taken = least & most

        @pl.when(taken)
        def _(skip=tiles_out * KEY_TILE):
            groups_from(skip)


def near(arrays):
    return [pltpu.with_memory_space_constraint(x, pltpu.VMEM) for x in arrays]


def far(arrays):
    return [pltpu.with_memory_space_constraint(x, pltpu.HBM) for x in arrays]


def per_device(queries, latent, w_uk, w_uv, doc_lengths):
    heads_dev, nope, rank = w_uk.shape
    vdim = w_uv.shape[2]
    tok = queries.shape[0]
    width = queries.shape[1] // heads_dev
    rows_per, lat = latent.shape
    n_seq, n_heads = lax.axis_size("seq"), lax.axis_size("heads")
    span = DOC_MOST // tok
    group = min(HEADS_GROUP, heads_dev)
    step = min(HEADS_STEP, heads_dev)
    rows = group * tok // SUBS
    kpad = -(-lat // LANES) * LANES

    edge = TAIL_MOST if n_seq == 2 * span else 0
    win = DOC_MOST + (edge or tok)
    hbm = pl.BlockSpec(memory_space=pl.ANY)
    vmem = pl.BlockSpec(memory_space=pltpu.VMEM)
    joined_type = pltpu.VMEM((heads_dev // group, SUBS, rows, kpad), jnp.bfloat16)
    steps = heads_dev // step

    def absorb_call(part, joined, brings):
        base = steps * sum(PARTS[:part]) // sum(PARTS)
        count = steps * sum(PARTS[: part + 1]) // sum(PARTS) - base
        heads = count * step
        wuv_type = pltpu.VMEM(w_uv.shape, w_uv.dtype)
        return pl.pallas_call(
            functools.partial(absorb, tok, nope, width, rank, lat, base, joined is None, brings),
            grid=(count,),
            in_specs=[
                pl.BlockSpec((tok, step * width), lambda i: (0, base + i)),
                pl.BlockSpec((step, nope, rank), lambda i: (base + i, 0, 0)),
            ]
            + [vmem] * (joined is not None)
            + [hbm] * brings,
            out_specs=[vmem] * (1 + brings),
            out_shape=[joined_type] + [wuv_type] * brings,
            scratch_shapes=[pltpu.SemaphoreType.DMA] * brings,
            compiler_params=pltpu.CompilerParams(vmem_limit_bytes=24 * 1024 * 1024),
            cost_estimate=pl.CostEstimate(
                flops=2 * tok * heads * nope * rank, bytes_accessed=4 * heads * nope * rank, transcendentals=0
            ),
            input_output_aliases={} if joined is None else {2: 0},
        )(*far([queries, w_uk]), *([] if joined is None else near([joined])), *far([w_uv] * brings))

    def swap(x, turn):
        return lax.ppermute(x, "heads", [(c, (c + turn) % n_heads) for c in range(n_heads)])

    bits = [latent] + [swap(latent, turn) for turn in range(1, n_heads)]
    if edge:
        source = span * n_heads - 1
        target = (span + span // 2 - 1) * n_heads
        bits += [lax.ppermute(latent, ("seq", "heads"), [(source, target + c)]) for c in range(n_heads)]
    (joined,) = absorb_call(0, None, False)
    *bits, joined = lax.optimization_barrier((*bits, joined))
    own = pl.pallas_call(
        functools.partial(pack, n_heads, edge),
        in_specs=[vmem] * len(bits),
        out_specs=vmem,
        out_shape=pltpu.VMEM((tok + edge, lat), latent.dtype),
        compiler_params=pltpu.CompilerParams(vmem_limit_bytes=2 * 1024 * 1024),
    )(*near(bits))
    direct = []
    if edge:
        for ks in partners(span, n_heads):
            pairs = [
                (t * n_heads + c, (t ^ k) * n_heads + c) for c, k in enumerate(ks) if k for t in range(n_seq)
            ]
            direct.append(lax.ppermute(own, ("seq", "heads"), pairs))
    else:
        per = -(-span // n_heads)
        for n in range(per):
            pairs = []
            for c in range(n_heads):
                shift = 1 + c * per + n
                if shift <= span:
                    pairs += [(t * n_heads + c, (t + shift) * n_heads + c) for t in range(n_seq - shift)]
            direct.append(lax.ppermute(own, ("seq", "heads"), pairs))
    own, joined = lax.optimization_barrier((own, joined))
    joined, w_uv_near = absorb_call(1, joined, True)
    *direct, joined = lax.optimization_barrier((*direct, joined))
    pieces = list(direct)
    for turn in range(1, n_heads):
        pieces += [swap(x, turn) for x in direct]
    if len(PARTS) > 2:
        (joined,) = absorb_call(2, joined, False)

    wpad = -(-win // KEY_TILE) * KEY_TILE
    plan = (
        n_heads, tok, rank, lat, vdim, win, wpad, span, doc_lengths.shape[0], width**-0.5 * math.log2(math.e),
        edge,
    )
    return pl.pallas_call(
        functools.partial(attend, plan),
        in_specs=[pl.BlockSpec(memory_space=pltpu.SMEM)] + [vmem] * (len(pieces) + 3),
        out_specs=vmem,
        out_shape=jax.ShapeDtypeStruct((tok, heads_dev * vdim), jnp.bfloat16),
        scratch_shapes=[
            pltpu.VMEM((win + tok, lat), jnp.bfloat16),
            pltpu.VMEM((kpad, wpad), jnp.bfloat16),
            pltpu.VMEM((tok, wpad), jnp.float32),
            pltpu.VMEM((rows, wpad), jnp.float32),
            pltpu.VMEM((rows, wpad), jnp.float32),
            pltpu.VMEM((rows, wpad), jnp.bfloat16),
            pltpu.VMEM((rows, wpad), jnp.bfloat16),
            pltpu.VMEM((group * tok, rank), jnp.bfloat16),
        ],
        compiler_params=pltpu.CompilerParams(vmem_limit_bytes=24 * 1024 * 1024),
    )(doc_lengths, *near([own, *pieces, joined, w_uv_near]))


def solution(mesh):
    return jax.shard_map(
        per_device,
        mesh=mesh,
        in_specs=(
            P("seq", "heads"),
            P(("seq", "heads"), None),
            P("heads", None, None),
            P("heads", None, None),
            P(),
        ),
        out_specs=P("seq", "heads"),
        check_vma=False,
    )
```

time: 61.3 us -> 54.2 us (0.88)
  the two profiles are of different devices: /device:TPU:3 before, /device:TPU:29 now
where the time goes in v3:
time: 54.2 us; the launch traced here: 54 us
  Pallas kernels  42.9 us (79%)
  starting transfers between devices  9.56 us (18%)
  waiting for transfers between devices  1.47 us (3%)
    pallas_call x1, Pallas kernels, per_device(): pl.pallas_call(functools.partial(attend, plan), in_specs=[pl.BlockSpec(me...  33.2 us
    pallas_call x2, Pallas kernels, absorb_call(): pl.pallas_call(functools.partial(absorb, tok, nope, width, rank, lat, bas...  9.67 us
    ppermute x4, starting transfers between devices, per_device(): direct.append(lax.ppermute(own, ('seq', 'heads'), pairs))  5.81 us
    ppermute x5, starting transfers between devices, swap(): lax.ppermute(x, 'heads', [(c, (c + turn) % n_heads) for c in range(n_head...  2.44 us
    ppermute x5, waiting for transfers between devices, swap(): lax.ppermute(x, 'heads', [(c, (c + turn) % n_heads) for c in range(n_head...  1.45 us
    ppermute x2, starting transfers between devices, per_device(): lax.ppermute(latent, ('seq', 'heads'), [(source, target + c)])  1.32 us
  transfers between devices with their start and end apart: 11, of which 4 were waited for; matrix products, arithmetic and copies ran while one was open for 0% of the time, Pallas kernels for 18%

profile of v3, /device:TPU:29, one launch (start us, length us, event | category | flops | bytes accessed | tf_op | source)
XLA Modules:
  0.0 54.0 jit_solution(3729677992947095901)
XLA Ops:
  0.0 0.0 copy-start
  0.0 0.7 %collective-permute-start = (bf16[64,576]{1,0:T(8,128)(2,1)}, bf16[64,576]{1,0:T(8,128)(2,1)S(1)}, u32[]{:S(2)}, u32[]{:S(2)}) collective-permute-start(bf16[64,576]{1,0:T(8,128)(2,1)} %refs_0_.3), channel_id=1, source_target_pairs={{0,1},{1,0},{2,3},{3,2},{4,5},{5,4},{6,7},{7,6},{8,9},{9,8},{10,11... | collective-permute-start | bytes 221192 | tf_op jit(solution)/shard_map/ppermute | solution.py:275
  0.7 0.7 %collective-permute-start.1 = (bf16[64,576]{1,0:T(8,128)(2,1)}, bf16[64,576]{1,0:T(8,128)(2,1)S(1)}, u32[]{:S(2)}, u32[]{:S(2)}) collective-permute-start(bf16[64,576]{1,0:T(8,128)(2,1)} %refs_0_.3), channel_id=1, source_target_pairs={{15,22}} | collective-permute-start | bytes 221192 | tf_op jit(solution)/shard_map/ppermute | solution.py:281
  1.3 0.7 %collective-permute-start.2 = (bf16[64,576]{1,0:T(8,128)(2,1)}, bf16[64,576]{1,0:T(8,128)(2,1)S(1)}, u32[]{:S(2)}, u32[]{:S(2)}) collective-permute-start(bf16[64,576]{1,0:T(8,128)(2,1)} %refs_0_.3), channel_id=1, source_target_pairs={{15,23}} | collective-permute-start | bytes 221192 | tf_op jit(solution)/shard_map/ppermute | solution.py:281
  2.0 2.6 %shard_map.55.refs_2_ = bf16[8,4,256,640]{3,2,1,0:T(8,128)(2,1)S(1)} custom-call(bf16[128,12288]{1,0:T(8,128)(2,1)} %refs_0_.4, bf16[64,128,512]{2,1,0:T(8,128)(2,1)} %refs_1_.3), custom_call_target="tpu_custom_call" | custom-call | flops 268435456 | bytes 4194304 | tf_op jit(solution)/shard_map/pallas_call | solution.py:255
  4.6 0.0 collective-permute-done.refs_1_
  4.6 0.0 collective-permute-done.1.refs_2_
  4.6 0.0 collective-permute-done.2.refs_3_
  4.7 0.0 copy-done
  4.7 0.0 copy-start.1
  4.7 0.3 collective-permute-start.3
  5.0 2.2 %collective-permute-start.4 = (bf16[160,576]{1,0:T(8,128)(2,1)S(1)}, bf16[160,576]{1,0:T(8,128)(2,1)S(1)}, u32[]{:S(2)}, u32[]{:S(2)}) collective-permute-start(bf16[160,576]{1,0:T(8,128)(2,1)S(1)} %shard_map.56.refs_0_), channel_id=1, source_target_pairs={{0,8},{2,10},{4,12},{6,14},{8,0},{10,2},{12,4},{14,6},{16,24},{18,... | collective-permute-start | bytes 552968 | tf_op jit(solution)/shard_map/ppermute | solution.py:297
  7.2 2.7 %collective-permute-start.5 = (bf16[160,576]{1,0:T(8,128)(2,1)S(1)}, bf16[160,576]{1,0:T(8,128)(2,1)S(1)}, u32[]{:S(2)}, u32[]{:S(2)}) collective-permute-start(bf16[160,576]{1,0:T(8,128)(2,1)S(1)} %shard_map.56.refs_0_), channel_id=1, source_target_pairs={{0,10},{2,8},{4,14},{6,12},{8,2},{10,0},{12,6},{14,4},{16,26},{18,... | collective-permute-start | bytes 552968 | tf_op jit(solution)/shard_map/ppermute | solution.py:297
  9.9 0.7 %collective-permute-start.6 = (bf16[160,576]{1,0:T(8,128)(2,1)S(1)}, bf16[160,576]{1,0:T(8,128)(2,1)S(1)}, u32[]{:S(2)}, u32[]{:S(2)}) collective-permute-start(bf16[160,576]{1,0:T(8,128)(2,1)S(1)} %shard_map.56.refs_0_), channel_id=1, source_target_pairs={{0,14},{2,12},{4,10},{6,8},{8,6},{10,4},{12,2},{14,0},{16,30},{18,... | collective-permute-start | bytes 552968 | tf_op jit(solution)/shard_map/ppermute | solution.py:297
  10.5 7.1 %shard_map.57 = (bf16[8,4,256,640]{3,2,1,0:T(8,128)(2,1)S(1)}, bf16[64,512,128]{2,1,0:T(8,128)(2,1)S(1)}) custom-call(bf16[128,12288]{1,0:T(8,128)(2,1)} %refs_0_.4, bf16[64,128,512]{2,1,0:T(8,128)(2,1)} %refs_1_.3, bf16[8,4,256,640]{3,2,1,0:T(8,128)(2,1)S(1)} %shard_map.55.refs_2_, bf16[64,512,128]{2,1,0:T(8,128)(2,1)} %refs_3_.1), custom_call_target="tpu_custom_call", output_to_operand_aliasing={{0}: (2, {})} | custom-call | flops 805306368 | bytes 12582912 | tf_op jit(solution)/shard_map/pallas_call | solution.py:255
  17.6 0.0 collective-permute-done.3.refs_1_
  17.6 0.0 collective-permute-done.4.refs_2_
  17.6 0.0 collective-permute-done.5.refs_3_
  17.6 0.0 collective-permute-done.6.refs_4_
  17.6 1.2 %collective-permute-start.10 = (bf16[160,576]{1,0:T(8,128)(2,1)S(1)}, bf16[160,576]{1,0:T(8,128)(2,1)S(1)}, u32[]{:S(2)}, u32[]{:S(2)}) collective-permute-start(bf16[160,576]{1,0:T(8,128)(2,1)S(1)} %collective-permute-done.6.refs_4_), channel_id=1, source_target_pairs={{0,1},{1,0},{2,3},{3,2},{4,5},{5,4},{6,7},{7,6},{8,9},{9,8},{10,11... | collective-permute-start | bytes 552968 | tf_op jit(solution)/shard_map/ppermute | solution.py:275
  18.8 0.1 collective-permute-start.7
  18.9 0.4 collective-permute-start.8
  19.3 0.1 collective-permute-start.9
  19.4 0.5 collective-permute-done.10.refs_8_
  19.9 0.4 collective-permute-done.7.refs_5_
  20.3 0.3 collective-permute-done.8.refs_6_
  20.6 0.3 collective-permute-done.9.refs_7_
  20.9 0.0 copy-done.1
  20.9 33.2 %shard_map.58 = bf16[128,8192]{1,0:T(8,128)(2,1)} custom-call(s32[8]{0:T(128)S(1)} %copy-done.1, bf16[160,576]{1,0:T(8,128)(2,1)S(1)} %shard_map.56.refs_0_, bf16[160,576]{1,0:T(8,128)(2,1)S(1)} %collective-permute-done.3.refs_1_, bf16[160,576]{1,0:T(8,128)(2,1)S(1)} %collective-permute-done.4.refs_2_, bf16[160,576]{1,0:T(8,128)(2,1)S(1)} %collective-permute-done.5.refs_3_, ...), custom_call_target="tpu_custom_call" | custom-call | tf_op jit(solution)/shard_map/pallas_call | solution.py:321
  (1 shorter events, 0.0 us)
Async XLA Ops:
  0.0 4.7 %copy-start = (bf16[64,576]{1,0:T(8,128)(2,1)S(1)}, bf16[64,576]{1,0:T(8,128)(2,1)}, u32[]{:S(2)}) copy-start(bf16[64,576]{1,0:T(8,128)(2,1)} %refs_0_.3) | copy-start | bytes 221188
  0.0 4.6 %collective-permute-start = (bf16[64,576]{1,0:T(8,128)(2,1)}, bf16[64,576]{1,0:T(8,128)(2,1)S(1)}, u32[]{:S(2)}, u32[]{:S(2)}) collective-permute-start(bf16[64,576]{1,0:T(8,128)(2,1)} %refs_0_.3), channel_id=1, source_target_pairs={{0,1},{1,0},{2,3},{3,2},{4,5},{5,4},{6,7},{7,6},{8,9},{9,8},{10,11... | collective-permute-start | bytes 221192 | tf_op jit(solution)/shard_map/ppermute | solution.py:275
  0.7 4.0 %collective-permute-start.1 = (bf16[64,576]{1,0:T(8,128)(2,1)}, bf16[64,576]{1,0:T(8,128)(2,1)S(1)}, u32[]{:S(2)}, u32[]{:S(2)}) collective-permute-start(bf16[64,576]{1,0:T(8,128)(2,1)} %refs_0_.3), channel_id=1, source_target_pairs={{15,22}} | collective-permute-start | bytes 221192 | tf_op jit(solution)/shard_map/ppermute | solution.py:281
  1.3 3.3 %collective-permute-start.2 = (bf16[64,576]{1,0:T(8,128)(2,1)}, bf16[64,576]{1,0:T(8,128)(2,1)S(1)}, u32[]{:S(2)}, u32[]{:S(2)}) collective-permute-start(bf16[64,576]{1,0:T(8,128)(2,1)} %refs_0_.3), channel_id=1, source_target_pairs={{15,23}} | collective-permute-start | bytes 221192 | tf_op jit(solution)/shard_map/ppermute | solution.py:281
  4.7 16.2 %copy-start.1 = (s32[8]{0:T(128)S(1)}, s32[8]{0:T(128)}, u32[]{:S(2)}) copy-start(s32[8]{0:T(128)} %lengths.1) | copy-start | bytes 100
  4.7 12.9 %collective-permute-start.3 = (bf16[160,576]{1,0:T(8,128)(2,1)S(1)}, bf16[160,576]{1,0:T(8,128)(2,1)S(1)}, u32[]{:S(2)}, u32[]{:S(2)}) collective-permute-start(bf16[160,576]{1,0:T(8,128)(2,1)S(1)} %shard_map.56.refs_0_), channel_id=1, source_target_pairs={{0,2},{2,0},{4,6},{6,4},{8,10},{10,8},{12,14},{14,12},{16,18},{18,... | collective-permute-start | bytes 552968 | tf_op jit(solution)/shard_map/ppermute | solution.py:297
  5.0 12.6 %collective-permute-start.4 = (bf16[160,576]{1,0:T(8,128)(2,1)S(1)}, bf16[160,576]{1,0:T(8,128)(2,1)S(1)}, u32[]{:S(2)}, u32[]{:S(2)}) collective-permute-start(bf16[160,576]{1,0:T(8,128)(2,1)S(1)} %shard_map.56.refs_0_), channel_id=1, source_target_pairs={{0,8},{2,10},{4,12},{6,14},{8,0},{10,2},{12,4},{14,6},{16,24},{18,... | collective-permute-start | bytes 552968 | tf_op jit(solution)/shard_map/ppermute | solution.py:297
  7.2 10.4 %collective-permute-start.5 = (bf16[160,576]{1,0:T(8,128)(2,1)S(1)}, bf16[160,576]{1,0:T(8,128)(2,1)S(1)}, u32[]{:S(2)}, u32[]{:S(2)}) collective-permute-start(bf16[160,576]{1,0:T(8,128)(2,1)S(1)} %shard_map.56.refs_0_), channel_id=1, source_target_pairs={{0,10},{2,8},{4,14},{6,12},{8,2},{10,0},{12,6},{14,4},{16,26},{18,... | collective-permute-start | bytes 552968 | tf_op jit(solution)/shard_map/ppermute | solution.py:297
  9.9 7.8 %collective-permute-start.6 = (bf16[160,576]{1,0:T(8,128)(2,1)S(1)}, bf16[160,576]{1,0:T(8,128)(2,1)S(1)}, u32[]{:S(2)}, u32[]{:S(2)}) collective-permute-start(bf16[160,576]{1,0:T(8,128)(2,1)S(1)} %shard_map.56.refs_0_), channel_id=1, source_target_pairs={{0,14},{2,12},{4,10},{6,8},{8,6},{10,4},{12,2},{14,0},{16,30},{18,... | collective-permute-start | bytes 552968 | tf_op jit(solution)/shard_map/ppermute | solution.py:297
  17.6 2.3 %collective-permute-start.10 = (bf16[160,576]{1,0:T(8,128)(2,1)S(1)}, bf16[160,576]{1,0:T(8,128)(2,1)S(1)}, u32[]{:S(2)}, u32[]{:S(2)}) collective-permute-start(bf16[160,576]{1,0:T(8,128)(2,1)S(1)} %collective-permute-done.6.refs_4_), channel_id=1, source_target_pairs={{0,1},{1,0},{2,3},{3,2},{4,5},{5,4},{6,7},{7,6},{8,9},{9,8},{10,11... | collective-permute-start | bytes 552968 | tf_op jit(solution)/shard_map/ppermute | solution.py:275
  18.8 1.5 %collective-permute-start.7 = (bf16[160,576]{1,0:T(8,128)(2,1)S(1)}, bf16[160,576]{1,0:T(8,128)(2,1)S(1)}, u32[]{:S(2)}, u32[]{:S(2)}) collective-permute-start(bf16[160,576]{1,0:T(8,128)(2,1)S(1)} %collective-permute-done.3.refs_1_), channel_id=1, source_target_pairs={{0,1},{1,0},{2,3},{3,2},{4,5},{5,4},{6,7},{7,6},{8,9},{9,8},{10,11... | collective-permute-start | bytes 552968 | tf_op jit(solution)/shard_map/ppermute | solution.py:275
  18.9 1.7 %collective-permute-start.8 = (bf16[160,576]{1,0:T(8,128)(2,1)S(1)}, bf16[160,576]{1,0:T(8,128)(2,1)S(1)}, u32[]{:S(2)}, u32[]{:S(2)}) collective-permute-start(bf16[160,576]{1,0:T(8,128)(2,1)S(1)} %collective-permute-done.4.refs_2_), channel_id=1, source_target_pairs={{0,1},{1,0},{2,3},{3,2},{4,5},{5,4},{6,7},{7,6},{8,9},{9,8},{10,11... | collective-permute-start | bytes 552968 | tf_op jit(solution)/shard_map/ppermute | solution.py:275
  19.3 1.5 %collective-permute-start.9 = (bf16[160,576]{1,0:T(8,128)(2,1)S(1)}, bf16[160,576]{1,0:T(8,128)(2,1)S(1)}, u32[]{:S(2)}, u32[]{:S(2)}) collective-permute-start(bf16[160,576]{1,0:T(8,128)(2,1)S(1)} %collective-permute-done.5.refs_3_), channel_id=1, source_target_pairs={{0,1},{1,0},{2,3},{3,2},{4,5},{5,4},{6,7},{7,6},{8,9},{9,8},{10,11... | collective-permute-start | bytes 552968 | tf_op jit(solution)/shard_map/ppermute | solution.py:275

commit v4 on v3

--- a/solution.py
+++ b/solution.py
@@ -17,24 +17,15 @@
 HEADS_STEP = 16
 PARTS = (1, 3)
 LIGHT_TILES = 2
+OUT_PARTS = 4
+SOFT_ROWS = 16
 
 far_negative = -1e30
 
 
-def absorb(tok, nope, width, rank, lat, base, first, brings, *refs):
+def absorb(tok, nope, width, rank, lat, base, *refs):
     step = pl.program_id(0)
-    q_ref, wuk_ref, refs = refs[0], refs[1], refs[2:]
-    if not first:
-        refs = refs[1:]
-    if brings:
-        wuv_hbm, j_ref, wuv_ref, sem = refs
-        copy = pltpu.make_async_copy(wuv_hbm, wuv_ref, sem)
-
-        @pl.when(step == 0)
-        def _():
-            copy.start()
-    else:
-        (j_ref,) = refs
+    q_ref, wuk_ref, j_ref = refs[0], refs[1], refs[-1]
     sub_tok = tok // SUBS
     rows = j_ref.shape[2]
     group = rows // sub_tok
@@ -54,12 +45,6 @@
             j_ref[i, g, at : at + sub_tok, 0:rank] = absorbed[g * sub_tok : (g + 1) * sub_tok]
             j_ref[i, g, at : at + sub_tok, rank:kpad] = rope[g * sub_tok : (g + 1) * sub_tok]
 
-    if brings:
-
-        @pl.when(step == pl.num_programs(0) - 1)
-        def _():
-            copy.wait()
-
 
 def pack(n_heads, edge, *refs):
     o_ref = refs[-1]
@@ -76,7 +61,7 @@
 
 
 def partners(span, n_heads):
-    ks = sorted(range(1, span), key=lambda k: (k.bit_count(), k))
+    ks = sorted(range(1, span), key=lambda k: (-k.bit_count(), k))
     per = -(-len(ks) // n_heads)
     ks += [0] * (per * n_heads - len(ks))
     return [ks[n * n_heads : (n + 1) * n_heads] for n in range(per)]
@@ -87,13 +72,16 @@
     per = -(-(span - 1 if edge else span) // n_heads)
     own, refs = refs[0], refs[1:]
     pieces, refs = refs[: per * n_heads], refs[per * n_heads :]
-    j_ref, wuv_ref, o_ref, win_ref, kt_ref, bias_ref, s0, s1, p0, p1, att_ref = refs
+    j_ref, wuv_hbm, o_hbm, win_ref, kt_ref, bias_ref, s0, s1, p0, p1, att_ref, wuv_ref, o_ref, sem = refs
     s_refs, p_refs = (s0, s1), (p0, p1)
     sub_tok = tok // SUBS
     n_groups, _, rows, kpad = j_ref.shape
     group = rows // sub_tok
 
+    wuv_copy = pltpu.make_async_copy(wuv_hbm, wuv_ref, sem.at[0])
+    wuv_copy.start()
     seq, core = lax.axis_index("seq"), lax.axis_index("heads")
+    win_ref[win:, :] = jnp.zeros((win_ref.shape[0] - win, lat), win_ref.dtype)
     if edge:
         place = lax.rem(seq, span)
         held = [(own, place, place)]
@@ -147,57 +135,44 @@
             return [(c, min(KEY_TILE, n - c)) for c in range(skip, n, KEY_TILE)]
 
         def score(i, g):
-            s_ref = s_refs[g % 2]
-            top = None
             for c, w in tiles(g):
                 s = jnp.dot(j_ref[i, g], kt_ref[:, c : c + w], preferred_element_type=jnp.float32)
                 b = bias_ref[g * sub_tok : (g + 1) * sub_tok, c : c + w]
-                s = (s.reshape(group, sub_tok, w) + b[None]).reshape(rows, w)
-                s_ref[:, c : c + w] = s
-                for cc in range(0, w, LANES):
-                    m = s[:, cc : cc + LANES]
-                    top = m if top is None else jnp.maximum(top, m)
-            return jnp.max(top, axis=1, keepdims=True)
-
-        def soften(g, top):
+                s_refs[g % 2][:, c : c + w] = (s.reshape(group, sub_tok, w) + b[None]).reshape(rows, w)
+
+        def soften(g):
             s_ref, p_ref = s_refs[g % 2], p_refs[g % 2]
-            total = None
-            for c, w in tiles(g):
-                for cc in range(c, c + w, LANES):
-                    e = jnp.exp2((s_ref[:, cc : cc + LANES] - top) * factor)
-                    total = e if total is None else total + e
-                    p_ref[:, cc : cc + LANES] = e.astype(jnp.bfloat16)
-            return jnp.sum(total, axis=1, keepdims=True)
-
-        def mix(g, total):
-            p_ref = p_refs[g % 2]
-            n = reach(g)
-            mixed = None
-            for c in range(skip, n, DOC_MOST - skip):
-                e = min(n, c + DOC_MOST - skip)
-                part = jnp.dot(p_ref[:, c:e], win_ref[c:e, 0:rank], preferred_element_type=jnp.float32)
-                mixed = part if mixed is None else mixed + part
-            att = (mixed * (1.0 / total)).astype(jnp.bfloat16)
+            columns = [slice(cc, cc + LANES) for c, w in tiles(g) for cc in range(c, c + w, LANES)]
+            totals = []
+            for r in range(0, rows, SOFT_ROWS):
+                s = [s_ref[r : r + SOFT_ROWS, at] for at in columns]
+                top = jnp.max(functools.reduce(jnp.maximum, s), axis=1, keepdims=True)
+                e = [jnp.exp2((x - top) * factor) for x in s]
+                totals.append(jnp.sum(functools.reduce(jnp.add, e), axis=1, keepdims=True))
+                for at, x in zip(columns, e):
+                    p_ref[r : r + SOFT_ROWS, at] = x.astype(jnp.bfloat16)
+            return totals
+
+        def mix(i, g, totals):
+            n = tiles(g)[-1][0] + tiles(g)[-1][1]
+            mixed = jnp.dot(p_refs[g % 2][:, skip:n], win_ref[skip:n, 0:rank], preferred_element_type=jnp.float32)
+            mixed = mixed * (1.0 / jnp.concatenate(totals, axis=0))
+            att = mixed.astype(jnp.bfloat16)
             for h in range(group):
-                att_ref[h * tok + g * sub_tok : h * tok + (g + 1) * sub_tok, :] = att[h * sub_tok : (h + 1) * sub_tok]
-
-        def one_group(i, top):
+                at = pl.multiple_of((i * group + h) * tok + g * sub_tok, sub_tok)
+                att_ref[pl.ds(at, sub_tok), :] = att[h * sub_tok : (h + 1) * sub_tok]
+
+        def one_group(i, carry):
             for g in range(SUBS):
                 if g + 1 < SUBS:
-                    later = score(i, g + 1)
+                    score(i, g + 1)
                 else:
-                    later = score(jnp.minimum(i + 1, n_groups - 1), 0)
-                mix(g, soften(g, top))
-                top = later
-            for h in range(group):
-                out = jnp.dot(
-                    att_ref[h * tok : (h + 1) * tok, :], wuv_ref[i * group + h], preferred_element_type=jnp.float32
-                ).astype(o_ref.dtype)
-                at = pl.multiple_of((i * group + h) * vdim, vdim)
-                o_ref[:, pl.ds(at, vdim)] = out
-            return top
-
-        lax.fori_loop(0, n_groups, one_group, score(0, 0))
+                    score(jnp.minimum(i + 1, n_groups - 1), 0)
+                mix(i, g, soften(g))
+            return carry
+
+        score(0, 0)
+        lax.fori_loop(0, n_groups, one_group, 0)
 
     block_start, end = jnp.int32(0), jnp.int32(0)
     for d in range(n_docs):
@@ -218,6 +193,21 @@
         def _(skip=tiles_out * KEY_TILE):
             groups_from(skip)
 
+    wuv_copy.wait()
+    n_outs = sem.shape[0] - 1
+    outs = []
+    heads_out = n_groups * group // n_outs
+    for n in range(n_outs):
+        for h in range(n * heads_out, (n + 1) * heads_out):
+            o_ref[:, h * vdim : (h + 1) * vdim] = jnp.dot(
+                att_ref[h * tok : (h + 1) * tok, :], wuv_ref[h], preferred_element_type=jnp.float32
+            ).astype(o_ref.dtype)
+        part = pl.ds(n * heads_out * vdim, heads_out * vdim)
+        outs.append(pltpu.make_async_copy(o_ref.at[:, part], o_hbm.at[:, part], sem.at[1 + n]))
+        outs[-1].start()
+    for out in outs:
+        out.wait()
+
 
 def near(arrays):
     return [pltpu.with_memory_space_constraint(x, pltpu.VMEM) for x in arrays]
@@ -247,29 +237,26 @@
     joined_type = pltpu.VMEM((heads_dev // group, SUBS, rows, kpad), jnp.bfloat16)
     steps = heads_dev // step
 
-    def absorb_call(part, joined, brings):
+    def absorb_call(part, joined):
         base = steps * sum(PARTS[:part]) // sum(PARTS)
         count = steps * sum(PARTS[: part + 1]) // sum(PARTS) - base
         heads = count * step
-        wuv_type = pltpu.VMEM(w_uv.shape, w_uv.dtype)
         return pl.pallas_call(
-            functools.partial(absorb, tok, nope, width, rank, lat, base, joined is None, brings),
+            functools.partial(absorb, tok, nope, width, rank, lat, base),
             grid=(count,),
             in_specs=[
                 pl.BlockSpec((tok, step * width), lambda i: (0, base + i)),
                 pl.BlockSpec((step, nope, rank), lambda i: (base + i, 0, 0)),
             ]
-            + [vmem] * (joined is not None)
-            + [hbm] * brings,
-            out_specs=[vmem] * (1 + brings),
-            out_shape=[joined_type] + [wuv_type] * brings,
-            scratch_shapes=[pltpu.SemaphoreType.DMA] * brings,
+            + [vmem] * (joined is not None),
+            out_specs=vmem,
+            out_shape=joined_type,
             compiler_params=pltpu.CompilerParams(vmem_limit_bytes=24 * 1024 * 1024),
             cost_estimate=pl.CostEstimate(
                 flops=2 * tok * heads * nope * rank, bytes_accessed=4 * heads * nope * rank, transcendentals=0
             ),
             input_output_aliases={} if joined is None else {2: 0},
-        )(*far([queries, w_uk]), *([] if joined is None else near([joined])), *far([w_uv] * brings))
+        )(*far([queries, w_uk]), *([] if joined is None else near([joined])))
 
     def swap(x, turn):
         return lax.ppermute(x, "heads", [(c, (c + turn) % n_heads) for c in range(n_heads)])
@@ -279,7 +266,7 @@
         source = span * n_heads - 1
         target = (span + span // 2 - 1) * n_heads
         bits += [lax.ppermute(latent, ("seq", "heads"), [(source, target + c)]) for c in range(n_heads)]
-    (joined,) = absorb_call(0, None, False)
+    joined = absorb_call(0, None)
     *bits, joined = lax.optimization_barrier((*bits, joined))
     own = pl.pallas_call(
         functools.partial(pack, n_heads, edge),
@@ -305,13 +292,14 @@
                     pairs += [(t * n_heads + c, (t + shift) * n_heads + c) for t in range(n_seq - shift)]
             direct.append(lax.ppermute(own, ("seq", "heads"), pairs))
     own, joined = lax.optimization_barrier((own, joined))
-    joined, w_uv_near = absorb_call(1, joined, True)
-    *direct, joined = lax.optimization_barrier((*direct, joined))
+    joined = absorb_call(1, joined)
+    for n in range(len(direct)):
+        direct[n], joined = lax.optimization_barrier((direct[n], joined))
     pieces = list(direct)
     for turn in range(1, n_heads):
         pieces += [swap(x, turn) for x in direct]
     if len(PARTS) > 2:
-        (joined,) = absorb_call(2, joined, False)
+        joined = absorb_call(2, joined)
 
     wpad = -(-win // KEY_TILE) * KEY_TILE
     plan = (
@@ -320,8 +308,8 @@
     )
     return pl.pallas_call(
         functools.partial(attend, plan),
-        in_specs=[pl.BlockSpec(memory_space=pltpu.SMEM)] + [vmem] * (len(pieces) + 3),
-        out_specs=vmem,
+        in_specs=[pl.BlockSpec(memory_space=pltpu.SMEM)] + [vmem] * (len(pieces) + 2) + [hbm],
+        out_specs=hbm,
         out_shape=jax.ShapeDtypeStruct((tok, heads_dev * vdim), jnp.bfloat16),
         scratch_shapes=[
             pltpu.VMEM((win + tok, lat), jnp.bfloat16),
@@ -331,10 +319,13 @@
             pltpu.VMEM((rows, wpad), jnp.float32),
             pltpu.VMEM((rows, wpad), jnp.bfloat16),
             pltpu.VMEM((rows, wpad), jnp.bfloat16),
-            pltpu.VMEM((group * tok, rank), jnp.bfloat16),
+            pltpu.VMEM((heads_dev * tok, rank), jnp.bfloat16),
+            pltpu.VMEM(w_uv.shape, w_uv.dtype),
+            pltpu.VMEM((tok, heads_dev * vdim), jnp.bfloat16),
+            pltpu.SemaphoreType.DMA((1 + OUT_PARTS,)),
         ],
-        compiler_params=pltpu.CompilerParams(vmem_limit_bytes=24 * 1024 * 1024),
-    )(doc_lengths, *near([own, *pieces, joined, w_uv_near]))
+        compiler_params=pltpu.CompilerParams(vmem_limit_bytes=40 * 1024 * 1024),
+    )(doc_lengths, *near([own, *pieces, joined]), *far([w_uv]))
 
 
 def solution(mesh):

time: 54.2 us -> 52.4 us (0.967)
  Pallas kernels: 42.9 us -> 39.9 us
  waiting for transfers between devices: 1.47 us -> 2.96 us
    pallas_call x2, Pallas kernels: 9.67 us -> 7.87 us  [absorb_call(): pl.pallas_call(functools.partial(absorb, tok, nope, width, rank, lat, bas...]
    ppermute x4, waiting for transfers between devices: 0.01 us -> 1.42 us  [per_device(): direct.append(lax.ppermute(own, ('seq', 'heads'), pairs))]
    pallas_call x1, Pallas kernels: 33.2 us -> 32 us  [per_device(): pl.pallas_call(functools.partial(attend, plan), in_specs=[pl.BlockSpec(me...]
  transfers between devices with their start and end apart: 11 -> 11, of which waited for: 4 -> 5; matrix products, arithmetic and copies ran while one was open for 0% -> 0% of each run, Pallas kernels for 18% -> 15%
where the time goes in v4:
time: 52.4 us; the launch traced here: 52.2 us
  Pallas kernels  39.9 us (76%)
  starting transfers between devices  9.2 us (18%)
  waiting for transfers between devices  2.96 us (6%)
    pallas_call x1, Pallas kernels, per_device(): pl.pallas_call(functools.partial(attend, plan), in_specs=[pl.BlockSpec(me...  32 us
    pallas_call x2, Pallas kernels, absorb_call(): pl.pallas_call(functools.partial(absorb, tok, nope, width, rank, lat, bas...  7.87 us
    ppermute x4, starting transfers between devices, per_device(): direct.append(lax.ppermute(own, ('seq', 'heads'), pairs))  5.73 us
    ppermute x5, starting transfers between devices, swap(): lax.ppermute(x, 'heads', [(c, (c + turn) % n_heads) for c in range(n_head...  2.15 us
    ppermute x5, waiting for transfers between devices, swap(): lax.ppermute(x, 'heads', [(c, (c + turn) % n_heads) for c in range(n_head...  1.53 us
    ppermute x4, waiting for transfers between devices, per_device(): direct.append(lax.ppermute(own, ('seq', 'heads'), pairs))  1.42 us
    ppermute x2, starting transfers between devices, per_device(): lax.ppermute(latent, ('seq', 'heads'), [(source, target + c)])  1.32 us
  transfers between devices with their start and end apart: 11, of which 5 were waited for; matrix products, arithmetic and copies ran while one was open for 0% of the time, Pallas kernels for 15%

profile of v4, /device:TPU:29, one launch (start us, length us, event | category | flops | bytes accessed | tf_op | source)
XLA Modules:
  0.0 52.2 jit_solution(10770268815933851862)
XLA Ops:
  0.0 0.0 copy-start
  0.0 0.7 %collective-permute-start = (bf16[64,576]{1,0:T(8,128)(2,1)}, bf16[64,576]{1,0:T(8,128)(2,1)S(1)}, u32[]{:S(2)}, u32[]{:S(2)}) collective-permute-start(bf16[64,576]{1,0:T(8,128)(2,1)} %refs_0_.3), channel_id=1, source_target_pairs={{0,1},{1,0},{2,3},{3,2},{4,5},{5,4},{6,7},{7,6},{8,9},{9,8},{10,11... | collective-permute-start | bytes 221192 | tf_op jit(solution)/shard_map/ppermute | solution.py:262
  0.7 0.7 %collective-permute-start.1 = (bf16[64,576]{1,0:T(8,128)(2,1)}, bf16[64,576]{1,0:T(8,128)(2,1)S(1)}, u32[]{:S(2)}, u32[]{:S(2)}) collective-permute-start(bf16[64,576]{1,0:T(8,128)(2,1)} %refs_0_.3), channel_id=1, source_target_pairs={{15,22}} | collective-permute-start | bytes 221192 | tf_op jit(solution)/shard_map/ppermute | solution.py:268
  1.3 0.7 %collective-permute-start.2 = (bf16[64,576]{1,0:T(8,128)(2,1)}, bf16[64,576]{1,0:T(8,128)(2,1)S(1)}, u32[]{:S(2)}, u32[]{:S(2)}) collective-permute-start(bf16[64,576]{1,0:T(8,128)(2,1)} %refs_0_.3), channel_id=1, source_target_pairs={{15,23}} | collective-permute-start | bytes 221192 | tf_op jit(solution)/shard_map/ppermute | solution.py:268
  2.0 2.6 %shard_map.55.refs_2_ = bf16[8,4,256,640]{3,2,1,0:T(8,128)(2,1)S(1)} custom-call(bf16[128,12288]{1,0:T(8,128)(2,1)} %refs_0_.4, bf16[64,128,512]{2,1,0:T(8,128)(2,1)} %refs_1_.3), custom_call_target="tpu_custom_call" | custom-call | flops 268435456 | bytes 4194304 | tf_op jit(solution)/shard_map/pallas_call | solution.py:244
  4.6 0.0 collective-permute-done.refs_1_
  4.6 0.0 collective-permute-done.1.refs_2_
  4.6 0.0 collective-permute-done.2.refs_3_
  4.7 0.0 copy-done
  4.7 0.0 copy-start.1
  4.7 1.2 %collective-permute-start.3 = (bf16[160,576]{1,0:T(8,128)(2,1)S(1)}, bf16[160,576]{1,0:T(8,128)(2,1)S(1)}, u32[]{:S(2)}, u32[]{:S(2)}) collective-permute-start(bf16[160,576]{1,0:T(8,128)(2,1)S(1)} %shard_map.56.refs_0_), channel_id=1, source_target_pairs={{0,14},{2,12},{4,10},{6,8},{8,6},{10,4},{12,2},{14,0},{16,30},{18,... | collective-permute-start | bytes 552968 | tf_op jit(solution)/shard_map/ppermute | solution.py:284
  5.9 3.8 %collective-permute-start.4 = (bf16[160,576]{1,0:T(8,128)(2,1)S(1)}, bf16[160,576]{1,0:T(8,128)(2,1)S(1)}, u32[]{:S(2)}, u32[]{:S(2)}) collective-permute-start(bf16[160,576]{1,0:T(8,128)(2,1)S(1)} %shard_map.56.refs_0_), channel_id=1, source_target_pairs={{0,10},{2,8},{4,14},{6,12},{8,2},{10,0},{12,6},{14,4},{16,26},{18,... | collective-permute-start | bytes 552968 | tf_op jit(solution)/shard_map/ppermute | solution.py:284
  9.8 0.0 collective-permute-start.5
  9.8 0.7 %collective-permute-start.6 = (bf16[160,576]{1,0:T(8,128)(2,1)S(1)}, bf16[160,576]{1,0:T(8,128)(2,1)S(1)}, u32[]{:S(2)}, u32[]{:S(2)}) collective-permute-start(bf16[160,576]{1,0:T(8,128)(2,1)S(1)} %shard_map.56.refs_0_), channel_id=1, source_target_pairs={{0,8},{2,10},{4,12},{6,14},{8,0},{10,2},{12,4},{14,6},{16,24},{18,... | collective-permute-start | bytes 552968 | tf_op jit(solution)/shard_map/ppermute | solution.py:284
  10.5 5.3 %shard_map.57.refs_9_ = bf16[8,4,256,640]{3,2,1,0:T(8,128)(2,1)S(1)} custom-call(bf16[128,12288]{1,0:T(8,128)(2,1)} %refs_0_.4, bf16[64,128,512]{2,1,0:T(8,128)(2,1)} %refs_1_.3, bf16[8,4,256,640]{3,2,1,0:T(8,128)(2,1)S(1)} %shard_map.55.refs_2_), custom_call_target="tpu_custom_call", output_to_operand_aliasing={{}: (2, {})} | custom-call | flops 805306368 | bytes 12582912 | tf_op jit(solution)/shard_map/pallas_call | solution.py:244
  15.7 0.0 collective-permute-done.3.refs_1_
  15.7 0.0 collective-permute-done.4.refs_2_
  15.8 1.4 %collective-permute-done.5.refs_3_ = bf16[160,576]{1,0:T(8,128)(2,1)S(1)} collective-permute-done((bf16[160,576]{1,0:T(8,128)(2,1)S(1)}, bf16[160,576]{1,0:T(8,128)(2,1)S(1)}, u32[]{:S(2)}, u32[]{:S(2)}) %collective-permute-start.5) | collective-permute-done | bytes 184352 | tf_op jit(solution)/shard_map/ppermute | solution.py:284
  17.2 0.0 collective-permute-done.6.refs_4_
  17.2 1.0 %collective-permute-start.10 = (bf16[160,576]{1,0:T(8,128)(2,1)S(1)}, bf16[160,576]{1,0:T(8,128)(2,1)S(1)}, u32[]{:S(2)}, u32[]{:S(2)}) collective-permute-start(bf16[160,576]{1,0:T(8,128)(2,1)S(1)} %collective-permute-done.6.refs_4_), channel_id=1, source_target_pairs={{0,1},{1,0},{2,3},{3,2},{4,5},{5,4},{6,7},{7,6},{8,9},{9,8},{10,11... | collective-permute-start | bytes 552968 | tf_op jit(solution)/shard_map/ppermute | solution.py:262
  18.1 0.0 collective-permute-start.9
  18.1 0.5 collective-permute-start.8
  18.6 0.0 collective-permute-start.7
  18.6 0.6 %collective-permute-done.10.refs_8_ = bf16[160,576]{1,0:T(8,128)(2,1)S(1)} collective-permute-done((bf16[160,576]{1,0:T(8,128)(2,1)S(1)}, bf16[160,576]{1,0:T(8,128)(2,1)S(1)}, u32[]{:S(2)}, u32[]{:S(2)}) %collective-permute-start.10) | collective-permute-done | bytes 184352 | tf_op jit(solution)/shard_map/ppermute | solution.py:262
  19.2 0.4 collective-permute-done.9.refs_7_
  19.6 0.3 collective-permute-done.8.refs_6_
  19.9 0.3 collective-permute-done.7.refs_5_
  20.2 0.0 copy-done.1
  20.2 32.0 %shard_map.58 = bf16[128,8192]{1,0:T(8,128)(2,1)} custom-call(s32[8]{0:T(128)S(1)} %copy-done.1, bf16[160,576]{1,0:T(8,128)(2,1)S(1)} %shard_map.56.refs_0_, bf16[160,576]{1,0:T(8,128)(2,1)S(1)} %collective-permute-done.3.refs_1_, bf16[160,576]{1,0:T(8,128)(2,1)S(1)} %collective-permute-done.4.refs_2_, bf16[160,576]{1,0:T(8,128)(2,1)S(1)} %collective-permute-done.5.refs_3_, ...), custom_call_target="tpu_custom_call" | custom-call | tf_op jit(solution)/shard_map/pallas_call | solution.py:309
  (1 shorter events, 0.0 us)
Async XLA Ops:
  0.0 4.7 %copy-start = (bf16[64,576]{1,0:T(8,128)(2,1)S(1)}, bf16[64,576]{1,0:T(8,128)(2,1)}, u32[]{:S(2)}) copy-start(bf16[64,576]{1,0:T(8,128)(2,1)} %refs_0_.3) | copy-start | bytes 221188
  0.0 4.6 %collective-permute-start = (bf16[64,576]{1,0:T(8,128)(2,1)}, bf16[64,576]{1,0:T(8,128)(2,1)S(1)}, u32[]{:S(2)}, u32[]{:S(2)}) collective-permute-start(bf16[64,576]{1,0:T(8,128)(2,1)} %refs_0_.3), channel_id=1, source_target_pairs={{0,1},{1,0},{2,3},{3,2},{4,5},{5,4},{6,7},{7,6},{8,9},{9,8},{10,11... | collective-permute-start | bytes 221192 | tf_op jit(solution)/shard_map/ppermute | solution.py:262
  0.7 4.0 %collective-permute-start.1 = (bf16[64,576]{1,0:T(8,128)(2,1)}, bf16[64,576]{1,0:T(8,128)(2,1)S(1)}, u32[]{:S(2)}, u32[]{:S(2)}) collective-permute-start(bf16[64,576]{1,0:T(8,128)(2,1)} %refs_0_.3), channel_id=1, source_target_pairs={{15,22}} | collective-permute-start | bytes 221192 | tf_op jit(solution)/shard_map/ppermute | solution.py:268
  1.3 3.3 %collective-permute-start.2 = (bf16[64,576]{1,0:T(8,128)(2,1)}, bf16[64,576]{1,0:T(8,128)(2,1)S(1)}, u32[]{:S(2)}, u32[]{:S(2)}) collective-permute-start(bf16[64,576]{1,0:T(8,128)(2,1)} %refs_0_.3), channel_id=1, source_target_pairs={{15,23}} | collective-permute-start | bytes 221192 | tf_op jit(solution)/shard_map/ppermute | solution.py:268
  4.7 15.5 %copy-start.1 = (s32[8]{0:T(128)S(1)}, s32[8]{0:T(128)}, u32[]{:S(2)}) copy-start(s32[8]{0:T(128)} %lengths.1) | copy-start | bytes 100
  4.7 11.0 %collective-permute-start.3 = (bf16[160,576]{1,0:T(8,128)(2,1)S(1)}, bf16[160,576]{1,0:T(8,128)(2,1)S(1)}, u32[]{:S(2)}, u32[]{:S(2)}) collective-permute-start(bf16[160,576]{1,0:T(8,128)(2,1)S(1)} %shard_map.56.refs_0_), channel_id=1, source_target_pairs={{0,14},{2,12},{4,10},{6,8},{8,6},{10,4},{12,2},{14,0},{16,30},{18,... | collective-permute-start | bytes 552968 | tf_op jit(solution)/shard_map/ppermute | solution.py:284
  5.9 9.8 %collective-permute-start.4 = (bf16[160,576]{1,0:T(8,128)(2,1)S(1)}, bf16[160,576]{1,0:T(8,128)(2,1)S(1)}, u32[]{:S(2)}, u32[]{:S(2)}) collective-permute-start(bf16[160,576]{1,0:T(8,128)(2,1)S(1)} %shard_map.56.refs_0_), channel_id=1, source_target_pairs={{0,10},{2,8},{4,14},{6,12},{8,2},{10,0},{12,6},{14,4},{16,26},{18,... | collective-permute-start | bytes 552968 | tf_op jit(solution)/shard_map/ppermute | solution.py:284
  9.8 7.4 %collective-permute-start.5 = (bf16[160,576]{1,0:T(8,128)(2,1)S(1)}, bf16[160,576]{1,0:T(8,128)(2,1)S(1)}, u32[]{:S(2)}, u32[]{:S(2)}) collective-permute-start(bf16[160,576]{1,0:T(8,128)(2,1)S(1)} %shard_map.56.refs_0_), channel_id=1, source_target_pairs={{0,2},{2,0},{4,6},{6,4},{8,10},{10,8},{12,14},{14,12},{16,18},{18,... | collective-permute-start | bytes 552968 | tf_op jit(solution)/shard_map/ppermute | solution.py:284
  9.8 7.4 %collective-permute-start.6 = (bf16[160,576]{1,0:T(8,128)(2,1)S(1)}, bf16[160,576]{1,0:T(8,128)(2,1)S(1)}, u32[]{:S(2)}, u32[]{:S(2)}) collective-permute-start(bf16[160,576]{1,0:T(8,128)(2,1)S(1)} %shard_map.56.refs_0_), channel_id=1, source_target_pairs={{0,8},{2,10},{4,12},{6,14},{8,0},{10,2},{12,4},{14,6},{16,24},{18,... | collective-permute-start | bytes 552968 | tf_op jit(solution)/shard_map/ppermute | solution.py:284
  17.2 2.0 %collective-permute-start.10 = (bf16[160,576]{1,0:T(8,128)(2,1)S(1)}, bf16[160,576]{1,0:T(8,128)(2,1)S(1)}, u32[]{:S(2)}, u32[]{:S(2)}) collective-permute-start(bf16[160,576]{1,0:T(8,128)(2,1)S(1)} %collective-permute-done.6.refs_4_), channel_id=1, source_target_pairs={{0,1},{1,0},{2,3},{3,2},{4,5},{5,4},{6,7},{7,6},{8,9},{9,8},{10,11... | collective-permute-start | bytes 552968 | tf_op jit(solution)/shard_map/ppermute | solution.py:262
  18.1 1.5 %collective-permute-start.9 = (bf16[160,576]{1,0:T(8,128)(2,1)S(1)}, bf16[160,576]{1,0:T(8,128)(2,1)S(1)}, u32[]{:S(2)}, u32[]{:S(2)}) collective-permute-start(bf16[160,576]{1,0:T(8,128)(2,1)S(1)} %collective-permute-done.5.refs_3_), channel_id=1, source_target_pairs={{0,1},{1,0},{2,3},{3,2},{4,5},{5,4},{6,7},{7,6},{8,9},{9,8},{10,11... | collective-permute-start | bytes 552968 | tf_op jit(solution)/shard_map/ppermute | solution.py:262
  18.1 1.7 %collective-permute-start.8 = (bf16[160,576]{1,0:T(8,128)(2,1)S(1)}, bf16[160,576]{1,0:T(8,128)(2,1)S(1)}, u32[]{:S(2)}, u32[]{:S(2)}) collective-permute-start(bf16[160,576]{1,0:T(8,128)(2,1)S(1)} %collective-permute-done.4.refs_2_), channel_id=1, source_target_pairs={{0,1},{1,0},{2,3},{3,2},{4,5},{5,4},{6,7},{7,6},{8,9},{9,8},{10,11... | collective-permute-start | bytes 552968 | tf_op jit(solution)/shard_map/ppermute | solution.py:262
  18.6 1.5 %collective-permute-start.7 = (bf16[160,576]{1,0:T(8,128)(2,1)S(1)}, bf16[160,576]{1,0:T(8,128)(2,1)S(1)}, u32[]{:S(2)}, u32[]{:S(2)}) collective-permute-start(bf16[160,576]{1,0:T(8,128)(2,1)S(1)} %collective-permute-done.3.refs_1_), channel_id=1, source_target_pairs={{0,1},{1,0},{2,3},{3,2},{4,5},{5,4},{6,7},{7,6},{8,9},{9,8},{10,11... | collective-permute-start | bytes 552968 | tf_op jit(solution)/shard_map/ppermute | solution.py:262

commit v5 on v4

--- a/solution.py
+++ b/solution.py
@@ -14,10 +14,10 @@
 KEY_TILE = 256
 LANES = 128
 HEADS_GROUP = 8
-HEADS_STEP = 16
+HEADS_STEP = 8
 PARTS = (1, 3)
 LIGHT_TILES = 2
-OUT_PARTS = 4
+OUT_PARTS = 8
 SOFT_ROWS = 16
 
 far_negative = -1e30
@@ -162,17 +162,18 @@
                 at = pl.multiple_of((i * group + h) * tok + g * sub_tok, sub_tok)
                 att_ref[pl.ds(at, sub_tok), :] = att[h * sub_tok : (h + 1) * sub_tok]
 
-        def one_group(i, carry):
+        def one_group(i, carry, last=False):
             for g in range(SUBS):
                 if g + 1 < SUBS:
                     score(i, g + 1)
-                else:
-                    score(jnp.minimum(i + 1, n_groups - 1), 0)
+                elif not last:
+                    score(i + 1, 0)
                 mix(i, g, soften(g))
             return carry
 
         score(0, 0)
-        lax.fori_loop(0, n_groups, one_group, 0)
+        lax.fori_loop(0, n_groups - 1, one_group, 0)
+        one_group(n_groups - 1, 0, last=True)
 
     block_start, end = jnp.int32(0), jnp.int32(0)
     for d in range(n_docs):
@@ -261,11 +262,12 @@
     def swap(x, turn):
         return lax.ppermute(x, "heads", [(c, (c + turn) % n_heads) for c in range(n_heads)])
 
-    bits = [latent] + [swap(latent, turn) for turn in range(1, n_heads)]
+    edges = []
     if edge:
         source = span * n_heads - 1
         target = (span + span // 2 - 1) * n_heads
-        bits += [lax.ppermute(latent, ("seq", "heads"), [(source, target + c)]) for c in range(n_heads)]
+        edges = [lax.ppermute(latent, ("seq", "heads"), [(source, target + c)]) for c in range(n_heads)]
+    bits = [latent] + [swap(latent, turn) for turn in range(1, n_heads)] + edges
     joined = absorb_call(0, None)
     *bits, joined = lax.optimization_barrier((*bits, joined))
     own = pl.pallas_call(

time: 52.4 us -> 52 us (level)
  waiting for transfers between devices: 2.96 us -> 1.82 us
    ppermute x4, waiting for transfers between devices: 1.42 us -> 0.29 us  [per_device(): direct.append(lax.ppermute(own, ('seq', 'heads'), pairs))]
    pallas_call x2, Pallas kernels: 7.87 us -> 8.43 us  [absorb_call(): pl.pallas_call(functools.partial(absorb, tok, nope, width, rank, lat, bas...]
  transfers between devices with their start and end apart: 11 -> 11, of which waited for: 5 -> 5; matrix products, arithmetic and copies ran while one was open for 0% -> 0% of each run, Pallas kernels for 15% -> 16%
where the time goes in v5:
time: 52 us; the launch traced here: 51.6 us
  Pallas kernels  40.1 us (77%)
  starting transfers between devices  9.48 us (18%)
  waiting for transfers between devices  1.82 us (4%)
    pallas_call x1, Pallas kernels, per_device(): pl.pallas_call(functools.partial(attend, plan), in_specs=[pl.BlockSpec(me...  31.6 us
    pallas_call x2, Pallas kernels, absorb_call(): pl.pallas_call(functools.partial(absorb, tok, nope, width, rank, lat, bas...  8.43 us
    ppermute x4, starting transfers between devices, per_device(): direct.append(lax.ppermute(own, ('seq', 'heads'), pairs))  6.03 us
    ppermute x5, starting transfers between devices, swap(): lax.ppermute(x, 'heads', [(c, (c + turn) % n_heads) for c in range(n_head...  2.13 us
    ppermute x5, waiting for transfers between devices, swap(): lax.ppermute(x, 'heads', [(c, (c + turn) % n_heads) for c in range(n_head...  1.53 us
    ppermute x2, starting transfers between devices, per_device(): lax.ppermute(latent, ('seq', 'heads'), [(source, target + c)])  1.32 us
  transfers between devices with their start and end apart: 11, of which 5 were waited for; matrix products, arithmetic and copies ran while one was open for 0% of the time, Pallas kernels for 16%

profile of v5, /device:TPU:29, one launch (start us, length us, event | category | flops | bytes accessed | tf_op | source)
XLA Modules:
  0.0 51.6 jit_solution(5408766954715579404)
XLA Ops:
  0.0 0.0 copy-start
  0.0 0.7 %collective-permute-start = (bf16[64,576]{1,0:T(8,128)(2,1)}, bf16[64,576]{1,0:T(8,128)(2,1)S(1)}, u32[]{:S(2)}, u32[]{:S(2)}) collective-permute-start(bf16[64,576]{1,0:T(8,128)(2,1)} %refs_0_.3), channel_id=1, source_target_pairs={{0,1},{1,0},{2,3},{3,2},{4,5},{5,4},{6,7},{7,6},{8,9},{9,8},{10,11... | collective-permute-start | bytes 221192 | tf_op jit(solution)/shard_map/ppermute | solution.py:263
  0.7 0.7 %collective-permute-start.1 = (bf16[64,576]{1,0:T(8,128)(2,1)}, bf16[64,576]{1,0:T(8,128)(2,1)S(1)}, u32[]{:S(2)}, u32[]{:S(2)}) collective-permute-start(bf16[64,576]{1,0:T(8,128)(2,1)} %refs_0_.3), channel_id=1, source_target_pairs={{15,22}} | collective-permute-start | bytes 221192 | tf_op jit(solution)/shard_map/ppermute | solution.py:269
  1.3 0.7 %collective-permute-start.2 = (bf16[64,576]{1,0:T(8,128)(2,1)}, bf16[64,576]{1,0:T(8,128)(2,1)S(1)}, u32[]{:S(2)}, u32[]{:S(2)}) collective-permute-start(bf16[64,576]{1,0:T(8,128)(2,1)} %refs_0_.3), channel_id=1, source_target_pairs={{15,23}} | collective-permute-start | bytes 221192 | tf_op jit(solution)/shard_map/ppermute | solution.py:269
  2.0 2.3 %shard_map.55.refs_2_ = bf16[8,4,256,640]{3,2,1,0:T(8,128)(2,1)S(1)} custom-call(bf16[128,12288]{1,0:T(8,128)(2,1)} %refs_0_.4, bf16[64,128,512]{2,1,0:T(8,128)(2,1)} %refs_1_.3), custom_call_target="tpu_custom_call" | custom-call | flops 268435456 | bytes 4194304 | tf_op jit(solution)/shard_map/pallas_call | solution.py:245
  4.3 0.0 collective-permute-done.refs_1_
  4.3 0.0 collective-permute-done.1.refs_2_
  4.4 0.0 collective-permute-done.2.refs_3_
  4.4 0.0 copy-done
  4.4 0.0 copy-start.1
  4.4 1.2 %collective-permute-start.3 = (bf16[160,576]{1,0:T(8,128)(2,1)S(1)}, bf16[160,576]{1,0:T(8,128)(2,1)S(1)}, u32[]{:S(2)}, u32[]{:S(2)}) collective-permute-start(bf16[160,576]{1,0:T(8,128)(2,1)S(1)} %shard_map.56.refs_0_), channel_id=1, source_target_pairs={{0,14},{2,12},{4,10},{6,8},{8,6},{10,4},{12,2},{14,0},{16,30},{18,... | collective-permute-start | bytes 552968 | tf_op jit(solution)/shard_map/ppermute | solution.py:286
  5.6 4.2 %collective-permute-start.4 = (bf16[160,576]{1,0:T(8,128)(2,1)S(1)}, bf16[160,576]{1,0:T(8,128)(2,1)S(1)}, u32[]{:S(2)}, u32[]{:S(2)}) collective-permute-start(bf16[160,576]{1,0:T(8,128)(2,1)S(1)} %shard_map.56.refs_0_), channel_id=1, source_target_pairs={{0,10},{2,8},{4,14},{6,12},{8,2},{10,0},{12,6},{14,4},{16,26},{18,... | collective-permute-start | bytes 552968 | tf_op jit(solution)/shard_map/ppermute | solution.py:286
  9.8 0.0 collective-permute-start.5
  9.8 0.7 %collective-permute-start.6 = (bf16[160,576]{1,0:T(8,128)(2,1)S(1)}, bf16[160,576]{1,0:T(8,128)(2,1)S(1)}, u32[]{:S(2)}, u32[]{:S(2)}) collective-permute-start(bf16[160,576]{1,0:T(8,128)(2,1)S(1)} %shard_map.56.refs_0_), channel_id=1, source_target_pairs={{0,8},{2,10},{4,12},{6,14},{8,0},{10,2},{12,4},{14,6},{16,24},{18,... | collective-permute-start | bytes 552968 | tf_op jit(solution)/shard_map/ppermute | solution.py:286
  10.5 6.1 %shard_map.57.refs_9_ = bf16[8,4,256,640]{3,2,1,0:T(8,128)(2,1)S(1)} custom-call(bf16[128,12288]{1,0:T(8,128)(2,1)} %refs_0_.4, bf16[64,128,512]{2,1,0:T(8,128)(2,1)} %refs_1_.3, bf16[8,4,256,640]{3,2,1,0:T(8,128)(2,1)S(1)} %shard_map.55.refs_2_), custom_call_target="tpu_custom_call", output_to_operand_aliasing={{}: (2, {})} | custom-call | flops 805306368 | bytes 12582912 | tf_op jit(solution)/shard_map/pallas_call | solution.py:245
  16.6 0.0 collective-permute-done.3.refs_1_
  16.6 0.0 collective-permute-done.4.refs_2_
  16.6 0.3 collective-permute-done.5.refs_3_
  16.9 0.0 collective-permute-done.6.refs_4_
  16.9 0.9 %collective-permute-start.10 = (bf16[160,576]{1,0:T(8,128)(2,1)S(1)}, bf16[160,576]{1,0:T(8,128)(2,1)S(1)}, u32[]{:S(2)}, u32[]{:S(2)}) collective-permute-start(bf16[160,576]{1,0:T(8,128)(2,1)S(1)} %collective-permute-done.6.refs_4_), channel_id=1, source_target_pairs={{0,1},{1,0},{2,3},{3,2},{4,5},{5,4},{6,7},{7,6},{8,9},{9,8},{10,11... | collective-permute-start | bytes 552968 | tf_op jit(solution)/shard_map/ppermute | solution.py:263
  17.8 0.0 collective-permute-start.9
  17.8 0.5 collective-permute-start.8
  18.3 0.0 collective-permute-start.7
  18.3 0.6 %collective-permute-done.10.refs_8_ = bf16[160,576]{1,0:T(8,128)(2,1)S(1)} collective-permute-done((bf16[160,576]{1,0:T(8,128)(2,1)S(1)}, bf16[160,576]{1,0:T(8,128)(2,1)S(1)}, u32[]{:S(2)}, u32[]{:S(2)}) %collective-permute-start.10) | collective-permute-done | bytes 184352 | tf_op jit(solution)/shard_map/ppermute | solution.py:263
  18.9 0.4 collective-permute-done.9.refs_7_
  19.3 0.3 collective-permute-done.8.refs_6_
  19.6 0.3 collective-permute-done.7.refs_5_
  19.9 0.0 copy-done.1
  19.9 31.6 %shard_map.58 = bf16[128,8192]{1,0:T(8,128)(2,1)} custom-call(s32[8]{0:T(128)S(1)} %copy-done.1, bf16[160,576]{1,0:T(8,128)(2,1)S(1)} %shard_map.56.refs_0_, bf16[160,576]{1,0:T(8,128)(2,1)S(1)} %collective-permute-done.3.refs_1_, bf16[160,576]{1,0:T(8,128)(2,1)S(1)} %collective-permute-done.4.refs_2_, bf16[160,576]{1,0:T(8,128)(2,1)S(1)} %collective-permute-done.5.refs_3_, ...), custom_call_target="tpu_custom_call" | custom-call | tf_op jit(solution)/shard_map/pallas_call | solution.py:311
  (1 shorter events, 0.0 us)
Async XLA Ops:
  0.0 4.4 %copy-start = (bf16[64,576]{1,0:T(8,128)(2,1)S(1)}, bf16[64,576]{1,0:T(8,128)(2,1)}, u32[]{:S(2)}) copy-start(bf16[64,576]{1,0:T(8,128)(2,1)} %refs_0_.3) | copy-start | bytes 221188
  0.0 4.3 %collective-permute-start = (bf16[64,576]{1,0:T(8,128)(2,1)}, bf16[64,576]{1,0:T(8,128)(2,1)S(1)}, u32[]{:S(2)}, u32[]{:S(2)}) collective-permute-start(bf16[64,576]{1,0:T(8,128)(2,1)} %refs_0_.3), channel_id=1, source_target_pairs={{0,1},{1,0},{2,3},{3,2},{4,5},{5,4},{6,7},{7,6},{8,9},{9,8},{10,11... | collective-permute-start | bytes 221192 | tf_op jit(solution)/shard_map/ppermute | solution.py:263
  0.7 3.7 %collective-permute-start.1 = (bf16[64,576]{1,0:T(8,128)(2,1)}, bf16[64,576]{1,0:T(8,128)(2,1)S(1)}, u32[]{:S(2)}, u32[]{:S(2)}) collective-permute-start(bf16[64,576]{1,0:T(8,128)(2,1)} %refs_0_.3), channel_id=1, source_target_pairs={{15,22}} | collective-permute-start | bytes 221192 | tf_op jit(solution)/shard_map/ppermute | solution.py:269
  1.3 3.0 %collective-permute-start.2 = (bf16[64,576]{1,0:T(8,128)(2,1)}, bf16[64,576]{1,0:T(8,128)(2,1)S(1)}, u32[]{:S(2)}, u32[]{:S(2)}) collective-permute-start(bf16[64,576]{1,0:T(8,128)(2,1)} %refs_0_.3), channel_id=1, source_target_pairs={{15,23}} | collective-permute-start | bytes 221192 | tf_op jit(solution)/shard_map/ppermute | solution.py:269
  4.4 15.5 %copy-start.1 = (s32[8]{0:T(128)S(1)}, s32[8]{0:T(128)}, u32[]{:S(2)}) copy-start(s32[8]{0:T(128)} %lengths.1) | copy-start | bytes 100
  4.4 12.2 %collective-permute-start.3 = (bf16[160,576]{1,0:T(8,128)(2,1)S(1)}, bf16[160,576]{1,0:T(8,128)(2,1)S(1)}, u32[]{:S(2)}, u32[]{:S(2)}) collective-permute-start(bf16[160,576]{1,0:T(8,128)(2,1)S(1)} %shard_map.56.refs_0_), channel_id=1, source_target_pairs={{0,14},{2,12},{4,10},{6,8},{8,6},{10,4},{12,2},{14,0},{16,30},{18,... | collective-permute-start | bytes 552968 | tf_op jit(solution)/shard_map/ppermute | solution.py:286
  5.6 11.0 %collective-permute-start.4 = (bf16[160,576]{1,0:T(8,128)(2,1)S(1)}, bf16[160,576]{1,0:T(8,128)(2,1)S(1)}, u32[]{:S(2)}, u32[]{:S(2)}) collective-permute-start(bf16[160,576]{1,0:T(8,128)(2,1)S(1)} %shard_map.56.refs_0_), channel_id=1, source_target_pairs={{0,10},{2,8},{4,14},{6,12},{8,2},{10,0},{12,6},{14,4},{16,26},{18,... | collective-permute-start | bytes 552968 | tf_op jit(solution)/shard_map/ppermute | solution.py:286
  9.8 7.1 %collective-permute-start.5 = (bf16[160,576]{1,0:T(8,128)(2,1)S(1)}, bf16[160,576]{1,0:T(8,128)(2,1)S(1)}, u32[]{:S(2)}, u32[]{:S(2)}) collective-permute-start(bf16[160,576]{1,0:T(8,128)(2,1)S(1)} %shard_map.56.refs_0_), channel_id=1, source_target_pairs={{0,2},{2,0},{4,6},{6,4},{8,10},{10,8},{12,14},{14,12},{16,18},{18,... | collective-permute-start | bytes 552968 | tf_op jit(solution)/shard_map/ppermute | solution.py:286
  9.8 7.1 %collective-permute-start.6 = (bf16[160,576]{1,0:T(8,128)(2,1)S(1)}, bf16[160,576]{1,0:T(8,128)(2,1)S(1)}, u32[]{:S(2)}, u32[]{:S(2)}) collective-permute-start(bf16[160,576]{1,0:T(8,128)(2,1)S(1)} %shard_map.56.refs_0_), channel_id=1, source_target_pairs={{0,8},{2,10},{4,12},{6,14},{8,0},{10,2},{12,4},{14,6},{16,24},{18,... | collective-permute-start | bytes 552968 | tf_op jit(solution)/shard_map/ppermute | solution.py:286
  16.9 2.0 %collective-permute-start.10 = (bf16[160,576]{1,0:T(8,128)(2,1)S(1)}, bf16[160,576]{1,0:T(8,128)(2,1)S(1)}, u32[]{:S(2)}, u32[]{:S(2)}) collective-permute-start(bf16[160,576]{1,0:T(8,128)(2,1)S(1)} %collective-permute-done.6.refs_4_), channel_id=1, source_target_pairs={{0,1},{1,0},{2,3},{3,2},{4,5},{5,4},{6,7},{7,6},{8,9},{9,8},{10,11... | collective-permute-start | bytes 552968 | tf_op jit(solution)/shard_map/ppermute | solution.py:263
  17.8 1.5 %collective-permute-start.9 = (bf16[160,576]{1,0:T(8,128)(2,1)S(1)}, bf16[160,576]{1,0:T(8,128)(2,1)S(1)}, u32[]{:S(2)}, u32[]{:S(2)}) collective-permute-start(bf16[160,576]{1,0:T(8,128)(2,1)S(1)} %collective-permute-done.5.refs_3_), channel_id=1, source_target_pairs={{0,1},{1,0},{2,3},{3,2},{4,5},{5,4},{6,7},{7,6},{8,9},{9,8},{10,11... | collective-permute-start | bytes 552968 | tf_op jit(solution)/shard_map/ppermute | solution.py:263
  17.8 1.7 %collective-permute-start.8 = (bf16[160,576]{1,0:T(8,128)(2,1)S(1)}, bf16[160,576]{1,0:T(8,128)(2,1)S(1)}, u32[]{:S(2)}, u32[]{:S(2)}) collective-permute-start(bf16[160,576]{1,0:T(8,128)(2,1)S(1)} %collective-permute-done.4.refs_2_), channel_id=1, source_target_pairs={{0,1},{1,0},{2,3},{3,2},{4,5},{5,4},{6,7},{7,6},{8,9},{9,8},{10,11... | collective-permute-start | bytes 552968 | tf_op jit(solution)/shard_map/ppermute | solution.py:263
  18.3 1.5 %collective-permute-start.7 = (bf16[160,576]{1,0:T(8,128)(2,1)S(1)}, bf16[160,576]{1,0:T(8,128)(2,1)S(1)}, u32[]{:S(2)}, u32[]{:S(2)}) collective-permute-start(bf16[160,576]{1,0:T(8,128)(2,1)S(1)} %collective-permute-done.3.refs_1_), channel_id=1, source_target_pairs={{0,1},{1,0},{2,3},{3,2},{4,5},{5,4},{6,7},{7,6},{8,9},{9,8},{10,11... | collective-permute-start | bytes 552968 | tf_op jit(solution)/shard_map/ppermute | solution.py:263
